TPU v7x, 512 devices: a whole 4x8x8 slice. The times are simulated.
512 devices in a mesh: ctx: 128 (over z, y, core), head: 4 (over x).
Axes of the slice: x: 4, y: 8, z: 8, core: 2. Of those that a mesh axis runs over, the one named last changes fastest.
Arguments:
- features: bfloat16 [32768, 1024], P('ctx', 'head'), may hold values from -30 to 30
- w_qkv: bfloat16 [1024, 3, 1024], P(None, None, 'head'), may hold values from -1 to 1
- block_links: int32 [256, 9], P('ctx'), may hold values from -1 to 255, as said below
- d_out: bfloat16 [32768, 1024], P('ctx', 'head'), may hold values from -6 to 6
Outputs:
- attended: bfloat16 [32768, 1024], P('ctx', 'head')
- grad_features: bfloat16 [32768, 1024], P('ctx', 'head')
Inputs may be any that keep to these rules, and one draw needn't show every extreme that they name: `block_links`: row q lists in order the key blocks q - 1 to q + 1; then p - 1 to p + 1, p being the block on the previous coil turn; then n - 1 to n + 1, n being the block on the next coil turn. q - p and n - q lie between 3 and 5, and a distance of 5 occurs in both directions in every draw. A coil neighbour may be absent; the entries of an absent neighbour and entries outside the sequence are -1. Live entries of a row are distinct.
All inputs are finite; a program needn't handle non-finite values.
Results may differ from a plain program's by a relative error of at most 0.025.
Values may be sent and summed in bfloat16 or wider, within the bound.
A program may use at most 64 MiB of HBM per device.

v0:
```python
import jax
import jax.numpy as jnp
from jax import lax
from jax.sharding import PartitionSpec as P

HD = 128
BLK = 128
OMAX = 3


def shifted(value, axis, steps):
    count = lax.axis_size(axis)
    first, last = (max(0, -steps), min(count, count - steps))
    return lax.ppermute(value, axis, [(source, source + steps) for source in range(first, last)])


def rounded_terms(values):
    return lax.optimization_barrier(values.astype(jnp.bfloat16)).astype(jnp.float32)


def body(features, w_qkv, block_links, d_out):
    tok_rows = d_out.shape[0]
    local_width = w_qkv.shape[2]
    model_width = w_qkv.shape[0]
    resident_tiles = tok_rows // BLK
    heads_here = local_width // HD
    score_scale = HD ** (-0.5)
    w_flat = w_qkv.reshape(model_width, 3 * local_width)
    projected = jnp.dot(
        lax.all_gather(features, "head", axis=1, tiled=True),
        w_flat,
        preferred_element_type=jnp.float32,
    )
    projected = projected.astype(jnp.bfloat16)
    query_blocks = projected[:, :local_width].reshape(resident_tiles, BLK, heads_here, HD)
    pair_blocks = projected[:, local_width:].reshape(resident_tiles, BLK, 2 * local_width)
    lower_shards = []
    upper_shards = []
    for offset in range(1, OMAX + 1):
        for direction in (1, -1):
            arrived = shifted(pair_blocks, "ctx", direction * offset)
            if direction > 0:
                lower_shards.append(arrived)
            else:
                upper_shards.append(arrived)
    window_pairs = jnp.concatenate(
        list(reversed(lower_shards)) + [pair_blocks] + upper_shards, axis=0
    )
    extent = window_pairs.shape[0]
    own_start = OMAX * resident_tiles
    anchor = lax.axis_index("ctx") * resident_tiles - own_start
    live_slot = block_links >= 0
    slot_index = jnp.where(live_slot, block_links - anchor, own_start)
    drop_index = jnp.where(live_slot, block_links - anchor, extent)
    slots = block_links.shape[1]
    selected = window_pairs[slot_index].reshape(resident_tiles, slots * BLK, 2, heads_here, HD)
    lookup_rows = selected[:, :, 0]
    content_rows = selected[:, :, 1]
    key_mask = jnp.repeat(live_slot, BLK, axis=1)[:, None, None, :]
    grad_blocks = d_out.reshape(resident_tiles, BLK, heads_here, HD)
    scores = (
        jnp.einsum("iqhd,ikhd->ihqk", query_blocks, lookup_rows, preferred_element_type=jnp.float32)
        * score_scale
    )
    largest = jnp.max(jnp.where(key_mask, scores, -1e30), axis=-1, keepdims=True)
    exp_total = jnp.sum(jnp.where(key_mask, jnp.exp(scores - largest), 0.0), axis=-1, keepdims=True)
    normalized = jnp.where(key_mask, jnp.exp(scores - largest), 0.0) / exp_total
    softmax_share = normalized.astype(jnp.bfloat16)
    attended = jnp.einsum(
        "ihqk,ikhd->iqhd", softmax_share, content_rows, preferred_element_type=jnp.float32
    ).astype(jnp.bfloat16)
    row_dot = jnp.sum(grad_blocks.astype(jnp.float32) * attended.astype(jnp.float32), axis=-1)
    value_terms = jnp.einsum(
        "ihqk,iqhd->ikhd", softmax_share, grad_blocks, preferred_element_type=jnp.float32
    )
    probability_gradient = jnp.einsum(
        "iqhd,ikhd->ihqk", grad_blocks, content_rows, preferred_element_type=jnp.float32
    )
    recomputed = jnp.where(key_mask, jnp.exp(scores - largest), 0.0) / exp_total
    score_derivative = (
        recomputed * (probability_gradient - jnp.transpose(row_dot, (0, 2, 1))[:, :, :, None])
    ).astype(jnp.bfloat16)
    query_grad = (
        jnp.einsum(
            "ihqk,ikhd->iqhd", score_derivative, lookup_rows, preferred_element_type=jnp.float32
        )
        * score_scale
    )
    key_terms = (
        jnp.einsum(
            "ihqk,iqhd->ikhd", score_derivative, query_blocks, preferred_element_type=jnp.float32
        )
        * score_scale
    )
    flat_index = drop_index.reshape(-1)
    slot_owner = (flat_index[None, :] == jnp.arange(extent, dtype=jnp.int32)[:, None]).astype(
        jnp.float32
    )
    slot_terms = jnp.concatenate(
        [
            key_terms.reshape(resident_tiles * slots, BLK, local_width),
            value_terms.reshape(resident_tiles * slots, BLK, local_width),
        ],
        axis=2,
    )
    pair_grads = jnp.einsum(
        "es,sbc->ebc",
        slot_owner,
        slot_terms,
        precision=lax.Precision.HIGHEST,
        preferred_element_type=jnp.float32,
    )
    grad_total = rounded_terms(pair_grads[own_start : own_start + resident_tiles])
    for offset in range(1, OMAX + 1):
        for direction in (1, -1):
            domain_first_index = own_start + direction * offset * resident_tiles
            region = pair_grads[domain_first_index : domain_first_index + resident_tiles]
            arrived = shifted(region.astype(jnp.bfloat16), "ctx", direction * offset).astype(
                jnp.float32
            )
            grad_total = grad_total + arrived
    attended_all = attended.reshape(tok_rows, local_width)
    query_all = query_grad.reshape(tok_rows, local_width)
    grad_projected = jnp.concatenate(
        [query_all, grad_total.reshape(tok_rows, 2 * local_width)], axis=1
    ).astype(jnp.bfloat16)
    partial_sum = jnp.einsum(
        "tc,dc->td", grad_projected, w_flat, preferred_element_type=jnp.float32
    )
    grad_features = lax.psum_scatter(
        partial_sum.astype(jnp.bfloat16), "head", scatter_dimension=1, tiled=True
    )
    return (attended_all, grad_features)


def solution(mesh):
    return jax.shard_map(
        body,
        mesh=mesh,
        in_specs=(P("ctx", "head"), P(None, None, "head"), P("ctx", None), P("ctx", "head")),
        out_specs=(P("ctx", "head"), P("ctx", "head")),
        check_vma=False,
    )
```

profile of v0, /device:TPU:1, one launch (start us, length us, event | category | flops | bytes accessed | tf_op | source)
XLA Modules:
  0.0 182.5 jit_solution(3778253173048944143)
XLA Ops:
  7.2 11.3 %all_gather.3 = bf16[256,1024]{1,0:T(8,128)(2,1)S(1)} all-gather(bf16[256,256]{1,0:T(8,128)(2,1)} %param.4), channel_id=1, replica_groups=mesh['ctx'=128,'head'=4] {'head'}, dimensions={1}, use_global_device_ids=true | all-gather | bytes 655360 | tf_op jit(solution)/shard_map/all_gather | solution.py:30
  18.5 1.7 copy.33
  20.9 1.3 collective-permute-start.5
  23.5 12.7 %collective-permute-start.2 = (bf16[2,128,512]{2,1,0:T(8,128)(2,1)S(1)}, bf16[2,128,512]{2,1,0:T(8,128)(2,1)S(1)}, u32[]{:S(2)}, u32[]{:S(2)}) collective-permute-start(bf16[2,128,512]{2,1,0:T(8,128)(2,1)S(1)} %bitcast.64), channel_id=1, source_target_pairs={{0,4},{4,8},{8,12},{12,16},{16,20},{20,24},{24,28},{28,32},{32,36}... | collective-permute-start | bytes 786440 | tf_op jit(solution)/shard_map/ppermute | solution.py:14
  36.2 3.0 %collective-permute-start.1 = (bf16[2,128,512]{2,1,0:T(8,128)(2,1)S(1)}, bf16[2,128,512]{2,1,0:T(8,128)(2,1)}, u32[]{:S(2)}, u32[]{:S(2)}) collective-permute-start(bf16[2,128,512]{2,1,0:T(8,128)(2,1)S(1)} %bitcast.65), channel_id=1, source_target_pairs={{0,8},{4,12},{8,16},{12,20},{16,24},{20,28},{24,32},{28,36},{32,40... | collective-permute-start | bytes 786440 | tf_op jit(solution)/shard_map/ppermute | solution.py:14
  39.2 3.5 %collective-permute-start = (bf16[2,128,512]{2,1,0:T(8,128)(2,1)S(1)}, bf16[2,128,512]{2,1,0:T(8,128)(2,1)}, u32[]{:S(2)}, u32[]{:S(2)}) collective-permute-start(bf16[2,128,512]{2,1,0:T(8,128)(2,1)S(1)} %bitcast.66), channel_id=1, source_target_pairs={{0,12},{4,16},{8,20},{12,24},{16,28},{20,32},{24,36},{28,40},{32,4... | collective-permute-start | bytes 786440 | tf_op jit(solution)/shard_map/ppermute | solution.py:14
  43.4 9.7 %collective-permute-done = bf16[2,128,512]{2,1,0:T(8,128)(2,1)} collective-permute-done((bf16[2,128,512]{2,1,0:T(8,128)(2,1)S(1)}, bf16[2,128,512]{2,1,0:T(8,128)(2,1)}, u32[]{:S(2)}, u32[]{:S(2)}) %collective-permute-start) | collective-permute-done | bytes 262176 | tf_op jit(solution)/shard_map/ppermute | solution.py:14
  53.1 2.8 %collective-permute-start.3 = (bf16[2,128,512]{2,1,0:T(8,128)(2,1)S(1)}, bf16[2,128,512]{2,1,0:T(8,128)(2,1)S(1)}, u32[]{:S(2)}, u32[]{:S(2)}) collective-permute-start(bf16[2,128,512]{2,1,0:T(8,128)(2,1)S(1)} %bitcast.67), channel_id=1, source_target_pairs={{4,0},{8,4},{12,8},{16,12},{20,16},{24,20},{28,24},{32,28},{36,32}... | collective-permute-start | bytes 786440 | tf_op jit(solution)/shard_map/ppermute | solution.py:14
  55.9 1.7 constant_dynamic-update-slice_fusion.6
  57.6 1.7 constant_dynamic-update-slice_fusion.5
  62.9 2.2 %gather_fusion = bf16[18,128,512]{2,1,0:T(8,128)(2,1)S(1)} fusion(bf16[14,128,512]{2,1,0:T(8,128)(2,1)} %constant_dynamic-update-slice_fusion, s32[1024]{0:T(1024)S(1)} %pad_clamp_fusion), kind=kCustom, calls=%fused_computation | custom fusion | bytes 4718664 | tf_op jit(solution)/shard_map/gather | solution.py:56
  65.1 2.3 %reshape.43 = bf16[2,1152,2,2,128]{4,3,2,1,0:T(2,128)(2,1)} reshape(bf16[18,128,512]{2,1,0:T(8,128)(2,1)S(1)} %gather_fusion) | data formatting | bytes 4718592 | tf_op jit(solution)/shard_map/reshape | solution.py:56
  67.5 2.9 %fusion.42 = (bf16[2,1152,1,2,128]{4,3,2,1,0:T(2,128)(2,1)S(1)}, bf16[2,1152,1,2,128]{4,3,2,1,0:T(2,128)(2,1)S(1)}) fusion(bf16[2,1152,2,2,128]{4,3,2,1,0:T(2,128)(2,1)} %reshape.43), kind=kLoop, calls=%fused_computation.61 | loop fusion | bytes 4718592 | tf_op jit(solution)/shard_map/slice | solution.py:57
  70.4 2.8 %copy.56 = bf16[2,1152,1,2,128]{1,4,3,0,2:T(8,128)(2,1)} copy(bf16[2,1152,1,2,128]{4,3,2,1,0:T(2,128)(2,1)S(1)} %get-tuple-element.3) | data formatting | bytes 2359296
  77.2 1.6 fusion.16
  78.8 8.9 %copy.48 = f32[2,1152,2,128]{3,2,1,0:T(2,128)S(1)} copy(f32[2,1152,2,128]{3,1,2,0:T(8,128)S(1)} %convolution_bitcast_fusion) | data formatting | bytes 4718592 | tf_op jit(solution)/shard_map/ihqk,iqhd->ikhd/transpose | solution.py:73
  87.7 2.9 %reshape.49 = f32[18,128,256]{2,1,0:T(8,128)} reshape(f32[2,1152,2,128]{3,2,1,0:T(2,128)S(1)} %copy.48) | data formatting | bytes 4718592 | tf_op jit(solution)/shard_map/reshape | solution.py:102
  90.6 3.2 %copy.50 = f32[18,128,256]{2,0,1:T(8,128)S(1)} copy(f32[18,128,256]{2,1,0:T(8,128)} %reshape.49) | data formatting | bytes 4718592 | tf_op jit(solution)/shard_map/reshape | solution.py:102
  93.8 1.9 %fusion.13 = f32[2,1152,2,128]{1,3,2,0:T(8,128)} fusion(bf16[2,128,2,128]{1,3,2,0:T(8,128)(2,1)S(1)} %copy.44, bf16[2,2,128,1152]{3,2,1,0:T(8,128)(2,1)S(1)} %copy-done.4), kind=kOutput, calls=%fused_computation.15 | convolution fusion | flops 151584768 | bytes 3670016 | tf_op jit(solution)/shard_map/ihqk,iqhd->ikhd/dot_general | solution.py:90
  95.7 5.0 %copy.45 = f32[2,1152,2,128]{3,2,1,0:T(2,128)} copy(f32[2,1152,2,128]{1,3,2,0:T(8,128)} %fusion.13) | data formatting | bytes 4718592 | tf_op jit(solution)/shard_map/mul | solution.py:90
  100.7 4.1 %reshape.48 = f32[18,128,256]{2,1,0:T(8,128)} reshape(f32[2,1152,2,128]{3,2,1,0:T(2,128)} %copy.45) | data formatting | bytes 4718592 | tf_op jit(solution)/shard_map/reshape | solution.py:101
  104.8 3.1 %copy.49 = f32[18,128,256]{2,0,1:T(8,128)S(1)} copy(f32[18,128,256]{2,1,0:T(8,128)} %reshape.48) | data formatting | bytes 4718592 | tf_op jit(solution)/shard_map/reshape | solution.py:101
  107.9 3.7 %fusion.1 = bf16[14,128,512]{2,0,1:T(8,128)(2,1)S(1)} fusion(f32[18,128,256]{2,0,1:T(8,128)S(1)} %copy.50, f32[18,128,256]{2,0,1:T(8,128)S(1)} %copy.49, s32[18]{0:T(128)S(1)} %eq.15), kind=kOutput, calls=%fused_computation.2 | convolution fusion | flops 199360768 | bytes 6553672 | tf_op jit(solution)/shard_map/es,sbc->ebc/dot_general | solution.py:106
  112.9 1.4 collective-permute-start.11
  114.3 6.2 %collective-permute-start.10 = (bf16[2,128,512]{2,1,0:T(8,128)(2,1)S(1)}, bf16[2,128,512]{2,1,0:T(8,128)(2,1)}, u32[]{:S(2)}, u32[]{:S(2)}) collective-permute-start(bf16[2,128,512]{2,1,0:T(8,128)(2,1)S(1)} %get-tuple-element.6), channel_id=1, source_target_pairs={{0,12},{4,16},{8,20},{12,24},{16,28},{20,32},{24,36},{28,40},{32,4... | collective-permute-start | bytes 786440 | tf_op jit(solution)/shard_map/ppermute | solution.py:14
  121.8 4.7 %collective-permute-start.8 = (bf16[2,128,512]{2,1,0:T(8,128)(2,1)S(1)}, bf16[2,128,512]{2,1,0:T(8,128)(2,1)}, u32[]{:S(2)}, u32[]{:S(2)}) collective-permute-start(bf16[2,128,512]{2,1,0:T(8,128)(2,1)S(1)} %get-tuple-element.8), channel_id=1, source_target_pairs={{0,8},{4,12},{8,16},{12,20},{16,24},{20,28},{24,32},{28,36},{32,40... | collective-permute-start | bytes 786440 | tf_op jit(solution)/shard_map/ppermute | solution.py:14
  126.5 2.4 %collective-permute-start.7 = (bf16[2,128,512]{2,1,0:T(8,128)(2,1)S(1)}, bf16[2,128,512]{2,1,0:T(8,128)(2,1)}, u32[]{:S(2)}, u32[]{:S(2)}) collective-permute-start(bf16[2,128,512]{2,1,0:T(8,128)(2,1)S(1)} %get-tuple-element.9), channel_id=1, source_target_pairs={{4,0},{8,4},{12,8},{16,12},{20,16},{24,20},{28,24},{32,28},{36,32}... | collective-permute-start | bytes 786440 | tf_op jit(solution)/shard_map/ppermute | solution.py:14
  128.9 3.2 %collective-permute-start.6 = (bf16[2,128,512]{2,1,0:T(8,128)(2,1)S(1)}, bf16[2,128,512]{2,1,0:T(8,128)(2,1)}, u32[]{:S(2)}, u32[]{:S(2)}) collective-permute-start(bf16[2,128,512]{2,1,0:T(8,128)(2,1)S(1)} %get-tuple-element.10), channel_id=1, source_target_pairs={{0,4},{4,8},{8,12},{12,16},{16,20},{20,24},{24,28},{28,32},{32,36}... | collective-permute-start | bytes 786440 | tf_op jit(solution)/shard_map/ppermute | solution.py:14
  134.6 2.8 %collective-permute-done.6 = bf16[2,128,512]{2,1,0:T(8,128)(2,1)} collective-permute-done((bf16[2,128,512]{2,1,0:T(8,128)(2,1)S(1)}, bf16[2,128,512]{2,1,0:T(8,128)(2,1)}, u32[]{:S(2)}, u32[]{:S(2)}) %collective-permute-start.6) | collective-permute-done | bytes 262176 | tf_op jit(solution)/shard_map/ppermute | solution.py:14
  137.4 1.5 add_convert_fusion
  138.9 1.4 convolution_convert_fusion
  141.2 34.5 %reduce-scatter.2.cloned.1.call-done = bf16[256,256]{1,0:T(8,128)(2,1)} async-done(((bf16[256,1024]{1,0:T(8,128)(2,1)}), bf16[256,256]{1,0:T(8,128)(2,1)}) %reduce-scatter.2.cloned.1.call-update) | async-done | bytes 131088 | tf_op jit(solution)/shard_map/reduce_scatter | solution.py:130
  (64 shorter events, 15.9 us)
Async XLA Ops:
  7.2 168.5 %reduce-scatter.2.cloned.1.call-start = ((), (), s32[]{:S(2)}) async-start(), calls=%async_computation.1 | async-start | bytes 655360 | tf_op jit(solution)/shard_map/reduce_scatter | solution.py:130
  20.2 22.8 %copy-start.2 = (bf16[1024,3,256]{0,2,1:T(8,128)(2,1)}, bf16[1024,3,256]{0,2,1:T(8,128)(2,1)S(1)}, u32[]{:S(2)}) copy-start(bf16[1024,3,256]{0,2,1:T(8,128)(2,1)S(1)} %copy.33) | copy-start | bytes 4718596
  20.2 22.5 %copy-start.9 = (s32[2,9]{1,0:T(2,128)S(1)}, s32[2,9]{1,0:T(2,128)}, u32[]{:S(2)}) copy-start(s32[2,9]{1,0:T(2,128)} %param.6) | copy-start | bytes 220
  20.2 22.8 %copy-start.7 = (bf16[256,256]{1,0:T(8,128)(2,1)S(1)}, bf16[256,256]{1,0:T(8,128)(2,1)}, u32[]{:S(2)}) copy-start(bf16[256,256]{1,0:T(8,128)(2,1)} %param.7) | copy-start | bytes 393220
  20.9 41.3 %collective-permute-start.5 = (bf16[2,128,512]{2,1,0:T(8,128)(2,1)S(1)}, bf16[2,128,512]{2,1,0:T(8,128)(2,1)S(1)}, u32[]{:S(2)}, u32[]{:S(2)}) collective-permute-start(bf16[2,128,512]{2,1,0:T(8,128)(2,1)S(1)} %bitcast.62), channel_id=1, source_target_pairs={{12,0},{16,4},{20,8},{24,12},{28,16},{32,20},{36,24},{40,28},{44,3... | collective-permute-start | bytes 786440 | tf_op jit(solution)/shard_map/ppermute | solution.py:14
  22.2 39.3 %collective-permute-start.4 = (bf16[2,128,512]{2,1,0:T(8,128)(2,1)S(1)}, bf16[2,128,512]{2,1,0:T(8,128)(2,1)S(1)}, u32[]{:S(2)}, u32[]{:S(2)}) collective-permute-start(bf16[2,128,512]{2,1,0:T(8,128)(2,1)S(1)} %bitcast.63), channel_id=1, source_target_pairs={{8,0},{12,4},{16,8},{20,12},{24,16},{28,20},{32,24},{36,28},{40,32... | collective-permute-start | bytes 786440 | tf_op jit(solution)/shard_map/ppermute | solution.py:14
  23.5 35.7 %collective-permute-start.2 = (bf16[2,128,512]{2,1,0:T(8,128)(2,1)S(1)}, bf16[2,128,512]{2,1,0:T(8,128)(2,1)S(1)}, u32[]{:S(2)}, u32[]{:S(2)}) collective-permute-start(bf16[2,128,512]{2,1,0:T(8,128)(2,1)S(1)} %bitcast.64), channel_id=1, source_target_pairs={{0,4},{4,8},{8,12},{12,16},{16,20},{20,24},{24,28},{28,32},{32,36}... | collective-permute-start | bytes 786440 | tf_op jit(solution)/shard_map/ppermute | solution.py:14
  36.2 21.3 %collective-permute-start.1 = (bf16[2,128,512]{2,1,0:T(8,128)(2,1)S(1)}, bf16[2,128,512]{2,1,0:T(8,128)(2,1)}, u32[]{:S(2)}, u32[]{:S(2)}) collective-permute-start(bf16[2,128,512]{2,1,0:T(8,128)(2,1)S(1)} %bitcast.65), channel_id=1, source_target_pairs={{0,8},{4,12},{8,16},{12,20},{16,24},{20,28},{24,32},{28,36},{32,40... | collective-permute-start | bytes 786440 | tf_op jit(solution)/shard_map/ppermute | solution.py:14
  39.2 13.8 %collective-permute-start = (bf16[2,128,512]{2,1,0:T(8,128)(2,1)S(1)}, bf16[2,128,512]{2,1,0:T(8,128)(2,1)}, u32[]{:S(2)}, u32[]{:S(2)}) collective-permute-start(bf16[2,128,512]{2,1,0:T(8,128)(2,1)S(1)} %bitcast.66), channel_id=1, source_target_pairs={{0,12},{4,16},{8,20},{12,24},{16,28},{20,32},{24,36},{28,40},{32,4... | collective-permute-start | bytes 786440 | tf_op jit(solution)/shard_map/ppermute | solution.py:14
  53.1 7.7 %collective-permute-start.3 = (bf16[2,128,512]{2,1,0:T(8,128)(2,1)S(1)}, bf16[2,128,512]{2,1,0:T(8,128)(2,1)S(1)}, u32[]{:S(2)}, u32[]{:S(2)}) collective-permute-start(bf16[2,128,512]{2,1,0:T(8,128)(2,1)S(1)} %bitcast.67), channel_id=1, source_target_pairs={{4,0},{8,4},{12,8},{16,12},{20,16},{24,20},{28,24},{32,28},{36,32}... | collective-permute-start | bytes 786440 | tf_op jit(solution)/shard_map/ppermute | solution.py:14
  70.4 3.4 %copy-start = (bf16[2,1152,1,2,128]{4,3,2,1,0:T(2,128)(2,1)}, bf16[2,1152,1,2,128]{4,3,2,1,0:T(2,128)(2,1)S(1)}, u32[]{:S(2)}) copy-start(bf16[2,1152,1,2,128]{4,3,2,1,0:T(2,128)(2,1)S(1)} %get-tuple-element.2) | copy-start | bytes 3538948
  74.6 1.3 copy-start.6
  90.6 3.2 %copy-start.4 = (bf16[2,2,128,1152]{3,2,1,0:T(8,128)(2,1)S(1)}, bf16[2,2,128,1152]{3,2,1,0:T(8,128)(2,1)}, u32[]{:S(2)}) copy-start(bf16[2,2,128,1152]{3,2,1,0:T(8,128)(2,1)} %fusion.16) | copy-start | bytes 3538948
  112.6 19.4 %copy-start.1 = (bf16[2,1152,1,2,128]{4,3,2,1,0:T(2,128)(2,1)S(1)}, bf16[2,1152,1,2,128]{4,3,2,1,0:T(2,128)(2,1)}, u32[]{:S(2)}) copy-start(bf16[2,1152,1,2,128]{4,3,2,1,0:T(2,128)(2,1)} %copy-done) | copy-start | bytes 3538948
  112.7 19.4 %copy-start.5 = (bf16[2,2,128,1152]{3,2,1,0:T(8,128)(2,1)S(1)}, bf16[2,2,128,1152]{3,2,1,0:T(8,128)(2,1)}, u32[]{:S(2)}) copy-start(bf16[2,2,128,1152]{3,2,1,0:T(8,128)(2,1)} %fusion.16) | copy-start | bytes 3538948
  112.9 16.0 %collective-permute-start.11 = (bf16[2,128,512]{2,1,0:T(8,128)(2,1)S(1)}, bf16[2,128,512]{2,1,0:T(8,128)(2,1)S(1)}, u32[]{:S(2)}, u32[]{:S(2)}) collective-permute-start(bf16[2,128,512]{2,1,0:T(8,128)(2,1)S(1)} %get-tuple-element.5), channel_id=1, source_target_pairs={{12,0},{16,4},{20,8},{24,12},{28,16},{32,20},{36,24},{40,28},{44,3... | collective-permute-start | bytes 786440 | tf_op jit(solution)/shard_map/ppermute | solution.py:14
  114.3 20.3 %collective-permute-start.10 = (bf16[2,128,512]{2,1,0:T(8,128)(2,1)S(1)}, bf16[2,128,512]{2,1,0:T(8,128)(2,1)}, u32[]{:S(2)}, u32[]{:S(2)}) collective-permute-start(bf16[2,128,512]{2,1,0:T(8,128)(2,1)S(1)} %get-tuple-element.6), channel_id=1, source_target_pairs={{0,12},{4,16},{8,20},{12,24},{16,28},{20,32},{24,36},{28,40},{32,4... | collective-permute-start | bytes 786440 | tf_op jit(solution)/shard_map/ppermute | solution.py:14
  120.5 14.1 %collective-permute-start.9 = (bf16[2,128,512]{2,1,0:T(8,128)(2,1)S(1)}, bf16[2,128,512]{2,1,0:T(8,128)(2,1)}, u32[]{:S(2)}, u32[]{:S(2)}) collective-permute-start(bf16[2,128,512]{2,1,0:T(8,128)(2,1)S(1)} %get-tuple-element.7), channel_id=1, source_target_pairs={{8,0},{12,4},{16,8},{20,12},{24,16},{28,20},{32,24},{36,28},{40,32... | collective-permute-start | bytes 786440 | tf_op jit(solution)/shard_map/ppermute | solution.py:14
  121.8 12.8 %collective-permute-start.8 = (bf16[2,128,512]{2,1,0:T(8,128)(2,1)S(1)}, bf16[2,128,512]{2,1,0:T(8,128)(2,1)}, u32[]{:S(2)}, u32[]{:S(2)}) collective-permute-start(bf16[2,128,512]{2,1,0:T(8,128)(2,1)S(1)} %get-tuple-element.8), channel_id=1, source_target_pairs={{0,8},{4,12},{8,16},{12,20},{16,24},{20,28},{24,32},{28,36},{32,40... | collective-permute-start | bytes 786440 | tf_op jit(solution)/shard_map/ppermute | solution.py:14
  126.5 8.1 %collective-permute-start.7 = (bf16[2,128,512]{2,1,0:T(8,128)(2,1)S(1)}, bf16[2,128,512]{2,1,0:T(8,128)(2,1)}, u32[]{:S(2)}, u32[]{:S(2)}) collective-permute-start(bf16[2,128,512]{2,1,0:T(8,128)(2,1)S(1)} %get-tuple-element.9), channel_id=1, source_target_pairs={{4,0},{8,4},{12,8},{16,12},{20,16},{24,20},{28,24},{32,28},{36,32}... | collective-permute-start | bytes 786440 | tf_op jit(solution)/shard_map/ppermute | solution.py:14
  128.9 8.5 %collective-permute-start.6 = (bf16[2,128,512]{2,1,0:T(8,128)(2,1)S(1)}, bf16[2,128,512]{2,1,0:T(8,128)(2,1)}, u32[]{:S(2)}, u32[]{:S(2)}) collective-permute-start(bf16[2,128,512]{2,1,0:T(8,128)(2,1)S(1)} %get-tuple-element.10), channel_id=1, source_target_pairs={{0,4},{4,8},{8,12},{12,16},{16,20},{20,24},{24,28},{28,32},{32,36}... | collective-permute-start | bytes 786440 | tf_op jit(solution)/shard_map/ppermute | solution.py:14
  133.4 5.5 %copy-start.3 = (bf16[1024,3,256]{0,2,1:T(8,128)(2,1)S(1)}, bf16[1024,3,256]{0,2,1:T(8,128)(2,1)}, u32[]{:S(2)}) copy-start(bf16[1024,3,256]{0,2,1:T(8,128)(2,1)} %copy-done.2) | copy-start | bytes 4718596
  138.9 1.4 copy-start.8
Sparse Core Ops, SparseCore 0:
  140.5 35.1 reduce-scatter.1
where the time goes:
time: 184 us; the launch traced here: 183 us
  local copies, waits for them, and re-layouts  50.5 us (27%)
  waiting for transfers between devices  47.2 us (26%)
  starting transfers between devices  43.8 us (24%)
  between operations  14.4 us (8%)
  matrix products  13 us (7%)
  blocking collectives  11.3 us (6%)
  other arithmetic  2.32 us (1%)
    ppermute x12, starting transfers between devices, shifted(): lax.ppermute(value, axis, [(source, source + steps) for source in range(f...  43.8 us
    reduce_scatter x1, waiting for transfers between devices, body(): lax.psum_scatter(partial_sum.astype(jnp.bfloat16), 'head', scatter_dimens...  34.5 us
    ppermute x12, waiting for transfers between devices, shifted(): lax.ppermute(value, axis, [(source, source + steps) for source in range(f...  12.7 us
    unnamed x32, local copies, waits for them, and re-layouts  12.1 us
    all_gather x1, blocking collectives, body(): lax.all_gather(features, 'head', axis=1, tiled=True)  11.3 us
    transpose x1, local copies, waits for them, and re-layouts, body(): jnp.einsum('ihqk,iqhd->ikhd', softmax_share, grad_blocks, preferred_eleme...  8.88 us
    reshape x2, local copies, waits for them, and re-layouts, body(): key_terms.reshape(resident_tiles * slots, BLK, local_width)  7.22 us
    reshape x2, local copies, waits for them, and re-layouts, body(): value_terms.reshape(resident_tiles * slots, BLK, local_width)  6.11 us
  transfers between devices with their start and end apart: 13, of which 4 were waited for; matrix products, arithmetic and copies ran while one was open for 6% of the time, Pallas kernels for 0%

commit v1 on v0

v1 whole, which is shorter than its diff:
```python
import functools
import math

import jax
import jax.numpy as jnp
from jax import lax
from jax.experimental import pallas as pl
from jax.experimental.pallas import tpu as pltpu
from jax.sharding import PartitionSpec as P

MESH = pl.DeviceIdType.MESH
BLK = 128
HD = 128
SH = 256
SCALE = HD ** (-0.5)
C2 = SCALE * math.log2(math.e)
DEAD = -1e30
F32 = jnp.float32
BF16 = jnp.bfloat16
DO, K, V, Q = range(4)
PAD = 2
ROWS = 24
FAR = (-2, -1, 1, 2)
SOURCE = {0: (0, 1), 1: (1, 0), 2: (1, 1), 5: (2, 0), 6: (2, 1), 7: (3, 0)}


def dot(a, b):
    return jnp.dot(a, b, preferred_element_type=F32)


def dot_t(a, b):
    return lax.dot_general(a, b, (((1,), (1,)), ((), ())), preferred_element_type=F32)


def fold8(x, op):
    return op(x.reshape(x.shape[0] // 8, 8, x.shape[1]), axis=0)


def kernel(
    nctx,
    nhead,
    feat,
    w,
    links,
    dout,
    att,
    gout,
    F,
    W,
    ACC,
    WIN,
    OTH,
    BQ,
    S,
    DP,
    PB,
    DSB,
    KT,
    VT,
    MX,
    STO,
    STI,
    DKV,
    AST,
    GP,
    GST,
    RSO,
    RSI,
    OUT,
    loc,
    xs,
    xr,
    ws,
    wr,
    bs,
    br,
    ss,
    sr,
    as_,
    ar,
    gs,
    gr,
    rs,
    rr,
):
    g = lax.axis_index("ctx")
    hx = lax.axis_index("head")
    core = lax.rem(g, 2)
    oth = 1 - core
    chip = g // 2
    nchip = nctx // 2

    def at(distance, which):
        return (lax.rem(chip + distance + nchip, nchip) * 2 + which, hx)

    right = (g, lax.rem(hx + 1, nhead))
    left = (g, lax.rem(hx + nhead - 1, nhead))
    partner = at(0, oth)
    own_col = pl.ds(pl.multiple_of(core * HD, HD), HD)
    oth_col = pl.ds(pl.multiple_of(oth * HD, HD), HD)
    A, B = pl.ds(0, BLK), pl.ds(BLK, BLK)

    barrier = pltpu.get_barrier_semaphore()
    peers = [right, left, partner]
    peers += [at(d, k) for d in (1, -1) for k in (0, 1)]
    peers += [at(d, core) for d in (2, -2)]
    for peer in peers:
        pl.semaphore_signal(barrier, inc=1, device_id=peer, device_id_type=MESH)

    load_f = pltpu.make_async_copy(feat, F.at[0], loc.at[0])
    load_f.start()
    load_w = pltpu.make_async_copy(w, W, loc.at[1])
    load_w.start()
    load_d = pltpu.make_async_copy(dout.at[:, own_col], WIN.at[DO, 3 + core], loc.at[2])
    load_d.start()

    base = chip * 4 - 6 - PAD
    row = lax.broadcasted_iota(jnp.int32, (ROWS, BLK), 0)
    for r in range(2):
        live = None
        for j in range(9):
            entry = links[r, j]
            hit = row == jnp.where(entry >= 0, entry - base, -1)
            live = hit if live is None else live | hit
        BQ[core, :, r * BLK : (r + 1) * BLK] = jnp.where(live, 0.0, DEAD).astype(F32)

    started = []

    def send(src, dst, s_sem, r_sem, to):
        c = pltpu.make_async_remote_copy(
            src_ref=src,
            dst_ref=dst,
            send_sem=s_sem,
            recv_sem=r_sem,
            device_id=to,
            device_id_type=MESH,
        )
        c.start()
        started.append(c)

    def arrived(dst, s_sem, r_sem):
        pltpu.make_async_remote_copy(
            src_ref=dst,
            dst_ref=dst,
            send_sem=s_sem,
            recv_sem=r_sem,
            device_id=partner,
            device_id_type=MESH,
        ).wait_recv()

    def x_arrived(slot, half, n):
        arrived(F.at[slot, half], xs.at[n], xr.at[n])

    def win_arrived(kind, slot):
        arrived(WIN.at[kind, slot], ws.at[kind, 0], wr.at[kind, slot])

    def spread(kind, own, other):
        send(other, WIN.at[kind, 3 + core], ws.at[kind, 0], wr.at[kind, 3 + core], partner)
        for n, (d, slot) in enumerate(((1, 1 + core), (-1, 5 + core))):
            send(own, WIN.at[kind, slot], ws.at[kind, 1 + 2 * n], wr.at[kind, slot], at(d, core))
            send(other, WIN.at[kind, slot], ws.at[kind, 2 + 2 * n], wr.at[kind, slot], at(d, oth))

    def relay(kind):
        win_arrived(kind, 2)
        send(WIN.at[kind, 2], WIN.at[kind, 0], ws.at[kind, 5], wr.at[kind, 0], at(1, core))
        win_arrived(kind, 5)
        send(WIN.at[kind, 5], WIN.at[kind, 7], ws.at[kind, 6], wr.at[kind, 7], at(-1, core))

    pl.semaphore_wait(barrier, len(peers))

    send(feat.at[A], F.at[1, A], xs.at[0], xr.at[0], right)
    send(feat.at[B], F.at[2, B], xs.at[3], xr.at[3], left)
    send(feat.at[B], F.at[1, B], xs.at[1], xr.at[1], right)
    send(feat.at[A], F.at[2, A], xs.at[2], xr.at[2], left)
    send(BQ.at[core], BQ.at[core], bs.at[0], br.at[0], partner)
    spread(DO, dout.at[:, own_col], dout.at[:, oth_col])

    def w_rows(step):
        s = lax.rem(hx + step + nhead, nhead)
        return pl.ds(pl.multiple_of(s * SH, SH), SH)

    load_f.wait()
    load_w.wait()
    for i in range(3):
        ACC[i] = dot(F[0], W[i, w_rows(0), :])
    x_arrived(1, A, 0)
    send(F.at[1, A], F.at[3, A], xs.at[4], xr.at[4], right)
    x_arrived(2, B, 3)
    send(F.at[2, B], F.at[3, B], xs.at[5], xr.at[5], left)
    x_arrived(1, B, 1)
    for i in range(3):
        ACC[i] += dot(F[1], W[i, w_rows(-1), :])
    x_arrived(2, A, 2)
    for i in range(3):
        ACC[i] += dot(F[2], W[i, w_rows(1), :])
    relay(DO)
    x_arrived(3, A, 4)
    x_arrived(3, B, 5)
    for kind, i in ((K, 1), (V, 2), (Q, 0)):
        full = (ACC[i] + dot(F[3], W[i, w_rows(2), :])).astype(BF16)
        low, high = full[:, :HD], full[:, HD:]
        WIN[kind, 3 + core] = jnp.where(core == 0, low, high)
        OTH[kind] = jnp.where(core == 0, high, low)
        spread(kind, WIN.at[kind, 3 + core], OTH.at[kind])

    win_arrived(Q, 3 + oth)
    load_d.wait()
    win_arrived(DO, 3 + oth)
    arrived(BQ.at[oth], bs.at[0], br.at[0])
    MX[...] = jnp.full(MX.shape, -3e38, F32)

    def scores(s):
        for b in range(2):
            wb = 2 * s + b
            kb = WIN[K, s, b * BLK : (b + 1) * BLK, :]
            vb = WIN[V, s, b * BLK : (b + 1) * BLK, :]
            rows = slice(wb * BLK, (wb + 1) * BLK)
            for half in range(2):
                cols = slice(half * SH, (half + 1) * SH)
                x = dot_t(kb, WIN[Q, 3 + half]) * C2 + BQ[half, wb + PAD : wb + PAD + 1, :]
                S[rows, cols] = x
                MX[:, cols] = jnp.maximum(MX[:, cols], fold8(x, jnp.max))
                DP[rows, cols] = dot_t(vb, WIN[DO, 3 + half])
        KT[:, s * SH : (s + 1) * SH] = WIN[K, s].T
        VT[:, s * SH : (s + 1) * SH] = WIN[V, s].T

    win_arrived(K, 3 + oth)
    win_arrived(V, 3 + oth)
    scores(3)
    scores(4)
    relay(K)
    relay(V)
    scores(2)
    scores(5)
    relay(Q)
    for s in (1, 6, 0, 7):
        win_arrived(K, s)
        win_arrived(V, s)
        scores(s)

    m = jnp.max(MX[...], axis=0, keepdims=True)
    step = 32

    def totals(n, carry):
        l, rd = carry
        rows = pl.ds(pl.multiple_of(n * step, step), step)
        e = jnp.exp2(S[rows, :] - m)
        S[rows, :] = e
        return l + fold8(e, jnp.sum), rd + fold8(e * DP[rows, :], jnp.sum)

    zero = jnp.zeros((8, 2 * SH), F32)
    l, rd = lax.fori_loop(0, 8 * SH // step, totals, (zero, zero))
    il = 1.0 / jnp.sum(l, axis=0, keepdims=True)
    rd = jnp.sum(rd, axis=0, keepdims=True) * il
    for n, d in enumerate(FAR):
        STO[n, 0:1, :] = m
        STO[n, 1:2, :] = il
        STO[n, 2:3, :] = rd
        first = 6 + PAD + 4 * d
        for half in range(2):
            STO[n, 4:8, half * SH : (half + 1) * SH] = BQ[half, first : first + 4, :]
        send(STO.at[n], STI.at[3 - n], ss.at[n], sr.at[3 - n], at(d, core))

    def weights(n, carry):
        rows = pl.ds(pl.multiple_of(n * step, step), step)
        p = S[rows, :] * il
        PB[rows, :] = p.astype(BF16)
        DSB[rows, :] = (p * (DP[rows, :] - rd)).astype(BF16)
        return carry

    lax.fori_loop(0, 8 * SH // step, weights, 0)
    out = dot(VT[...], PB[...]).T.astype(BF16)
    AST[0] = out[:SH]
    AST[1] = out[SH:]
    send(AST.at[oth], att.at[:, own_col], as_.at[0], ar.at[0], partner)
    att_own = pltpu.make_async_copy(AST.at[core], att.at[:, own_col], loc.at[3])
    att_own.start()

    def hand_over(i, low, high):
        GP[i, :, own_col] = jnp.where(core == 0, low, high)
        GST[i] = jnp.where(core == 0, high, low)
        send(GST.at[i], GP.at[i, :, own_col], gs.at[i], gr.at[i], partner)

    dq = (dot(KT[...], DSB[...]) * SCALE).T.astype(BF16)
    hand_over(0, dq[:SH], dq[SH:])

    own = slice(3 * SH, 5 * SH)
    DKV[0] = dot(DSB[own, :], WIN[Q, 3:5].reshape(2 * SH, HD))
    DKV[1] = dot(PB[own, :], WIN[DO, 3:5].reshape(2 * SH, HD))
    seen = set()
    for s in (2, 5, 1, 6, 0, 7):
        n, half = SOURCE[s]
        if n not in seen:
            seen.add(n)
            arrived(STI.at[n], ss.at[n], sr.at[n])
        if s not in (2, 5):
            win_arrived(DO, s)
            win_arrived(Q, s)
        cols = slice(half * SH, (half + 1) * SH)
        sm, sil, srd = (STI[n, i : i + 1, cols] for i in range(3))
        qs, ds = WIN[Q, s], WIN[DO, s]
        for e in range(4):
            rows = slice((e % 2) * BLK, (e % 2 + 1) * BLK)
            x = dot_t(WIN[K, 3 + e // 2, rows, :], qs) * C2 + STI[n, 4 + e : 5 + e, cols]
            p = jnp.exp2(x - sm) * sil
            t = p * (dot_t(WIN[V, 3 + e // 2, rows, :], ds) - srd)
            rows = slice(e * BLK, (e + 1) * BLK)
            DKV[0, rows, :] += dot(t.astype(BF16), qs)
            DKV[1, rows, :] += dot(p.astype(BF16), ds)
    dk = (DKV[0] * SCALE).astype(BF16)
    hand_over(1, dk[:SH], dk[SH:])
    dv = DKV[1].astype(BF16)
    hand_over(2, dv[:SH], dv[SH:])

    for i in range(3):
        arrived(GP.at[i, :, oth_col], gs.at[i], gr.at[i])

    def partial(step):
        rows = w_rows(step)
        return sum(dot_t(GP[i], W[i, rows, :]) for i in range(3))

    def pass_on(n, to):
        send(RSO.at[n], RSI.at[n], rs.at[n], rr.at[n], to)

    def rs_arrived(n):
        arrived(RSI.at[n], rs.at[n], rr.at[n])
        return RSI[n].astype(F32)

    gx = partial(2)
    RSO[0] = gx[:BLK].astype(BF16)
    pass_on(0, right)
    RSO[1] = gx[BLK:].astype(BF16)
    pass_on(1, left)
    g_r = partial(1)
    RSO[2] = g_r[BLK:].astype(BF16)
    pass_on(2, right)
    g_l = partial(-1)
    RSO[3] = g_l[:BLK].astype(BF16)
    pass_on(3, left)
    RSO[4] = (g_r[:BLK] + rs_arrived(0)).astype(BF16)
    pass_on(4, right)
    RSO[5] = (g_l[BLK:] + rs_arrived(1)).astype(BF16)
    pass_on(5, left)
    g_o = partial(0)
    g_a = g_o[:BLK] + rs_arrived(3)
    g_b = g_o[BLK:] + rs_arrived(2)
    OUT[:BLK] = (g_a + rs_arrived(4)).astype(BF16)
    OUT[BLK:] = (g_b + rs_arrived(5)).astype(BF16)
    store = pltpu.make_async_copy(OUT, gout, loc.at[4])
    store.start()
    att_own.wait()
    arrived(att.at[:, oth_col], as_.at[0], ar.at[0])
    for c in started:
        c.wait_send()
    store.wait()


def solution(mesh):
    nctx, nhead = mesh.shape["ctx"], mesh.shape["head"]

    def body(features, w_qkv, block_links, d_out):
        w = jnp.transpose(w_qkv, (1, 0, 2))
        any_spec = pl.BlockSpec(memory_space=pl.ANY)
        dma = pltpu.SemaphoreType.DMA
        vmem = pltpu.VMEM
        return tuple(
            pl.pallas_call(
                functools.partial(kernel, nctx, nhead),
                out_shape=[
                    jax.ShapeDtypeStruct((SH, SH), BF16),
                    jax.ShapeDtypeStruct((SH, SH), BF16),
                ],
                in_specs=[
                    any_spec,
                    any_spec,
                    pl.BlockSpec(memory_space=pltpu.SMEM),
                    any_spec,
                ],
                out_specs=[any_spec, any_spec],
                scratch_shapes=[
                    vmem((4, SH, SH), BF16),
                    vmem((3, 1024, SH), BF16),
                    vmem((3, SH, SH), F32),
                    vmem((4, 8, SH, HD), BF16),
                    vmem((4, SH, HD), BF16),
                    vmem((2, ROWS, SH), F32),
                    vmem((8 * SH, 2 * SH), F32),
                    vmem((8 * SH, 2 * SH), F32),
                    vmem((8 * SH, 2 * SH), BF16),
                    vmem((8 * SH, 2 * SH), BF16),
                    vmem((HD, 8 * SH), BF16),
                    vmem((HD, 8 * SH), BF16),
                    vmem((8, 2 * SH), F32),
                    vmem((4, 8, 2 * SH), F32),
                    vmem((4, 8, 2 * SH), F32),
                    vmem((2, 2 * SH, HD), F32),
                    vmem((2, SH, HD), BF16),
                    vmem((3, SH, SH), BF16),
                    vmem((3, SH, HD), BF16),
                    vmem((6, BLK, SH), BF16),
                    vmem((6, BLK, SH), BF16),
                    vmem((SH, SH), BF16),
                    dma((5,)),
                    dma((6,)),
                    dma((6,)),
                    dma((4, 7)),
                    dma((4, 8)),
                    dma((1,)),
                    dma((1,)),
                    dma((4,)),
                    dma((4,)),
                    dma((1,)),
                    dma((1,)),
                    dma((3,)),
                    dma((3,)),
                    dma((6,)),
                    dma((6,)),
                ],
                compiler_params=pltpu.CompilerParams(
                    collective_id=0,
                    has_side_effects=True,
                    vmem_limit_bytes=48 * 1024 * 1024,
                ),
            )(features, w, block_links, d_out)
        )

    return jax.shard_map(
        body,
        mesh=mesh,
        in_specs=(P("ctx", "head"), P(None, None, "head"), P("ctx", None), P("ctx", "head")),
        out_specs=(P("ctx", "head"), P("ctx", "head")),
        check_vma=False,
    )
```

time: 184 us -> 64.1 us (0.35)
  Pallas kernels: 0 us -> 58 us
  waiting for transfers between devices: 47.2 us -> 0 us
  local copies, waits for them, and re-layouts: 50.5 us -> 5.2 us
  starting transfers between devices: 43.8 us -> 0 us
  between operations: 14.4 us -> 0.65 us
  matrix products: 13 us -> 0 us
  blocking collectives: 11.3 us -> 0 us
  other arithmetic: 2.32 us -> 0 us
    pallas_call x0 -> x1, Pallas kernels: none -> 58 us  [body(): pl.pallas_call(functools.partial(kernel, nctx, nhead), out_shape=[jax.Sha...]
    ppermute x12 -> x0, starting transfers between devices: 43.8 us -> none  [shifted(): lax.ppermute(value, axis, [(source, source + steps) for source in range(f...]
    reduce_scatter x1 -> x0, waiting for transfers between devices: 34.5 us -> none  [body(): lax.psum_scatter(partial_sum.astype(jnp.bfloat16), 'head', scatter_dimens...]
    reshape x9 -> x0, local copies, waits for them, and re-layouts: 16 us -> none  [the longest x2 7.22 us: body(): key_terms.reshape(resident_tiles * slots, BLK, local_width)]
    dot_general x9 -> x0, matrix products: 13 us -> none  [the longest x1 3.72 us: body(): jnp.einsum('es,sbc->ebc', slot_owner, slot_terms, precision=lax.Precision...]
    ppermute x12 -> x0, waiting for transfers between devices: 12.7 us -> none  [shifted(): lax.ppermute(value, axis, [(source, source + steps) for source in range(f...]
    all_gather x1 -> x0, blocking collectives: 11.3 us -> none  [body(): lax.all_gather(features, 'head', axis=1, tiled=True)]
    transpose x1 -> x0, local copies, waits for them, and re-layouts: 8.88 us -> none  [body(): jnp.einsum('ihqk,iqhd->ikhd', softmax_share, grad_blocks, preferred_eleme...]
  transfers between devices with their start and end apart: 13 -> 0, of which waited for: 4 -> 0; matrix products, arithmetic and copies ran while one was open for 6% -> 0% of each run, Pallas kernels for 0% -> 0%
where the time goes in v1:
time: 64.1 us; the launch traced here: 63.9 us
  Pallas kernels  58 us (90%)
  local copies, waits for them, and re-layouts  5.2 us (8%)
  between operations  0.65 us (1%)
    pallas_call x1, Pallas kernels, body(): pl.pallas_call(functools.partial(kernel, nctx, nhead), out_shape=[jax.Sha...  58 us
    unnamed x10, local copies, waits for them, and re-layouts  5.2 us

profile of v1, /device:TPU:1, one launch (start us, length us, event | category | flops | bytes accessed | tf_op | source)
XLA Modules:
  0.0 63.9 jit_solution(3294870126192531729)
XLA Ops:
  0.6 0.0 copy-start
  0.6 1.4 %copy-done = bf16[1024,3,256]{2,0,1:T(8,128)(2,1)S(1)} copy-done((bf16[1024,3,256]{2,0,1:T(8,128)(2,1)S(1)}, bf16[1024,3,256]{2,0,1:T(8,128)(2,1)}, u32[]{:S(2)}) %copy-start) | copy-done | bytes 1572888
  2.0 0.0 copy-start.1
  2.0 0.9 %copy-done.1 = bf16[256,256]{1,0:T(8,128)(2,1)S(1)} copy-done((bf16[256,256]{1,0:T(8,128)(2,1)S(1)}, bf16[256,256]{1,0:T(8,128)(2,1)}, u32[]{:S(2)}) %copy-start.1) | copy-done | bytes 131096
  2.9 0.0 copy-start.2
  2.9 0.9 %copy-done.2 = bf16[256,256]{1,0:T(8,128)(2,1)S(1)} copy-done((bf16[256,256]{1,0:T(8,128)(2,1)S(1)}, bf16[256,256]{1,0:T(8,128)(2,1)}, u32[]{:S(2)}) %copy-start.2) | copy-done | bytes 131096
  3.8 0.0 copy-start.3
  3.9 0.7 %copy-done.3 = s32[2,9]{1,0:T(2,128)S(1)} copy-done((s32[2,9]{1,0:T(2,128)S(1)}, s32[2,9]{1,0:T(2,128)}, u32[]{:S(2)}) %copy-start.3) | copy-done | bytes 96
  4.5 58.0 %shard_map.59 = (bf16[256,256]{1,0:T(8,128)(2,1)S(1)}, bf16[256,256]{1,0:T(8,128)(2,1)S(1)}) custom-call(bf16[256,256]{1,0:T(8,128)(2,1)S(1)} %copy-done.1, bf16[3,1024,256]{2,1,0:T(8,128)(2,1)S(1)} %bitcast.1, s32[2,9]{1,0:T(2,128)S(1)} %copy-done.3, bf16[256,256]{1,0:T(8,128)(2,1)S(1)} %copy-done.2), custom_call_target="tpu_custom_call" | custom-call | tf_op jit(solution)/shard_map/pallas_call | solution.py:367
  62.6 0.7 %copy.8 = bf16[256,256]{1,0:T(8,128)(2,1)} copy(bf16[256,256]{1,0:T(8,128)(2,1)S(1)} %get-tuple-element.4) | data formatting | bytes 262144
  63.2 0.7 %copy.9 = bf16[256,256]{1,0:T(8,128)(2,1)} copy(bf16[256,256]{1,0:T(8,128)(2,1)S(1)} %get-tuple-element.5) | data formatting | bytes 262144
Async XLA Ops:
  0.6 1.4 %copy-start = (bf16[1024,3,256]{2,0,1:T(8,128)(2,1)S(1)}, bf16[1024,3,256]{2,0,1:T(8,128)(2,1)}, u32[]{:S(2)}) copy-start(bf16[1024,3,256]{2,0,1:T(8,128)(2,1)} %param.5) | copy-start | bytes 4718596
  2.0 0.9 %copy-start.1 = (bf16[256,256]{1,0:T(8,128)(2,1)S(1)}, bf16[256,256]{1,0:T(8,128)(2,1)}, u32[]{:S(2)}) copy-start(bf16[256,256]{1,0:T(8,128)(2,1)} %feat.1) | copy-start | bytes 393220
  2.9 0.9 %copy-start.2 = (bf16[256,256]{1,0:T(8,128)(2,1)S(1)}, bf16[256,256]{1,0:T(8,128)(2,1)}, u32[]{:S(2)}) copy-start(bf16[256,256]{1,0:T(8,128)(2,1)} %dout.1) | copy-start | bytes 393220
  3.8 0.7 %copy-start.3 = (s32[2,9]{1,0:T(2,128)S(1)}, s32[2,9]{1,0:T(2,128)}, u32[]{:S(2)}) copy-start(s32[2,9]{1,0:T(2,128)} %links.1) | copy-start | bytes 220

commit v2 on v1

--- a/solution.py
+++ b/solution.py
@@ -67,9 +67,14 @@
     RSO,
     RSI,
     OUT,
+    FF,
+    FO,
+    LK,
     loc,
     xs,
     xr,
+    fs,
+    fr,
     ws,
     wr,
     bs,
@@ -89,6 +94,10 @@
     oth = 1 - core
     chip = g // 2
     nchip = nctx // 2
+    has = {-1: chip > 0, -2: chip > 1, 1: chip < nchip - 1, 2: chip < nchip - 2}
+    far_slot, far_oth = 7 * core, 7 * oth
+    far_here = ((core == 0) & has[-2]) | ((core == 1) & has[2])
+    far_there = ((core == 1) & has[-2]) | ((core == 0) & has[2])
 
     def at(distance, which):
         return (lax.rem(chip + distance + nchip, nchip) * 2 + which, hx)
@@ -100,12 +109,19 @@
     oth_col = pl.ds(pl.multiple_of(oth * HD, HD), HD)
     A, B = pl.ds(0, BLK), pl.ds(BLK, BLK)
 
+    load_l = pltpu.make_async_copy(links, LK, loc.at[5])
+    load_l.start()
     barrier = pltpu.get_barrier_semaphore()
-    peers = [right, left, partner]
-    peers += [at(d, k) for d in (1, -1) for k in (0, 1)]
-    peers += [at(d, core) for d in (2, -2)]
-    for peer in peers:
+    for peer in (right, left, partner):
         pl.semaphore_signal(barrier, inc=1, device_id=peer, device_id_type=MESH)
+    count = 3
+    for d in (1, -1, 2, -2):
+        count += 2 * has[d].astype(jnp.int32)
+
+        @pl.when(has[d])
+        def _():
+            for which in (0, 1):
+                pl.semaphore_signal(barrier, inc=1, device_id=at(d, which), device_id_type=MESH)
 
     load_f = pltpu.make_async_copy(feat, F.at[0], loc.at[0])
     load_f.start()
@@ -114,19 +130,30 @@
     load_d = pltpu.make_async_copy(dout.at[:, own_col], WIN.at[DO, 3 + core], loc.at[2])
     load_d.start()
 
+    for d, n, slots in ((-2, 0, (0,)), (-1, 1, (1, 2)), (1, 2, (5, 6)), (2, 3, (7,))):
+
+        @pl.when(jnp.logical_not(has[d]))
+        def _():
+            for slot in slots:
+                for kind in range(4):
+                    WIN[kind, slot] = jnp.zeros((SH, HD), BF16)
+            STI[n, 0:4] = jnp.zeros((4, 2 * SH), F32)
+            STI[n, 4:8] = jnp.full((4, 2 * SH), DEAD, F32)
+
     base = chip * 4 - 6 - PAD
     row = lax.broadcasted_iota(jnp.int32, (ROWS, BLK), 0)
+    load_l.wait()
     for r in range(2):
         live = None
         for j in range(9):
-            entry = links[r, j]
+            entry = LK[r, j]
             hit = row == jnp.where(entry >= 0, entry - base, -1)
             live = hit if live is None else live | hit
         BQ[core, :, r * BLK : (r + 1) * BLK] = jnp.where(live, 0.0, DEAD).astype(F32)
 
     started = []
 
-    def send(src, dst, s_sem, r_sem, to):
+    def send(src, dst, s_sem, r_sem, to, when=None):
         c = pltpu.make_async_remote_copy(
             src_ref=src,
             dst_ref=dst,
@@ -135,73 +162,118 @@
             device_id=to,
             device_id_type=MESH,
         )
-        c.start()
-        started.append(c)
-
-    def arrived(dst, s_sem, r_sem):
-        pltpu.make_async_remote_copy(
+        if when is None:
+            c.start()
+        else:
+            pl.when(when)(c.start)
+        started.append((c, when))
+
+    def arrived(dst, s_sem, r_sem, when=None):
+        c = pltpu.make_async_remote_copy(
             src_ref=dst,
             dst_ref=dst,
             send_sem=s_sem,
             recv_sem=r_sem,
             device_id=partner,
             device_id_type=MESH,
-        ).wait_recv()
-
-    def x_arrived(slot, half, n):
-        arrived(F.at[slot, half], xs.at[n], xr.at[n])
-
-    def win_arrived(kind, slot):
-        arrived(WIN.at[kind, slot], ws.at[kind, 0], wr.at[kind, slot])
+        )
+        if when is None:
+            c.wait_recv()
+        else:
+            pl.when(when)(c.wait_recv)
+
+    near = {0: has[-2], 1: has[-1], 2: has[-1], 5: has[1], 6: has[1], 7: has[2]}
+
+    def win_arrived(kind, slot, when=None):
+        if isinstance(slot, int):
+            when = near[slot]
+        arrived(WIN.at[kind, slot], ws.at[kind, 0], wr.at[kind, slot], when)
+
+    def to_partner(kind, slot, src, n, when=None):
+        send(src, WIN.at[kind, slot], ws.at[kind, n], wr.at[kind, slot], partner, when)
 
     def spread(kind, own, other):
-        send(other, WIN.at[kind, 3 + core], ws.at[kind, 0], wr.at[kind, 3 + core], partner)
+        to_partner(kind, 3 + core, other, 0)
         for n, (d, slot) in enumerate(((1, 1 + core), (-1, 5 + core))):
-            send(own, WIN.at[kind, slot], ws.at[kind, 1 + 2 * n], wr.at[kind, slot], at(d, core))
-            send(other, WIN.at[kind, slot], ws.at[kind, 2 + 2 * n], wr.at[kind, slot], at(d, oth))
+            send(own, WIN.at[kind, slot], ws.at[kind, 1 + 2 * n], wr.at[kind, slot], at(d, core), has[d])
+            send(other, WIN.at[kind, slot], ws.at[kind, 2 + 2 * n], wr.at[kind, slot], at(d, oth), has[d])
 
     def relay(kind):
-        win_arrived(kind, 2)
-        send(WIN.at[kind, 2], WIN.at[kind, 0], ws.at[kind, 5], wr.at[kind, 0], at(1, core))
-        win_arrived(kind, 5)
-        send(WIN.at[kind, 5], WIN.at[kind, 7], ws.at[kind, 6], wr.at[kind, 7], at(-1, core))
-
-    pl.semaphore_wait(barrier, len(peers))
-
-    send(feat.at[A], F.at[1, A], xs.at[0], xr.at[0], right)
-    send(feat.at[B], F.at[2, B], xs.at[3], xr.at[3], left)
-    send(feat.at[B], F.at[1, B], xs.at[1], xr.at[1], right)
-    send(feat.at[A], F.at[2, A], xs.at[2], xr.at[2], left)
-    send(BQ.at[core], BQ.at[core], bs.at[0], br.at[0], partner)
-    spread(DO, dout.at[:, own_col], dout.at[:, oth_col])
+        for n, (d, slot, to) in enumerate(((1, 2, 0), (-1, 5, 7))):
+            win_arrived(kind, slot)
+            both = has[1] & has[-1]
+            send(WIN.at[kind, slot], WIN.at[kind, to], ws.at[kind, 5 + n], wr.at[kind, to], at(d, core), both)
+
+    class Gather:
+        def __init__(self, src, buf, s, r, when):
+            self.src, self.buf, self.s, self.r, self.when = src, buf, s, r, when
+
+        def begin(self):
+            src, buf = self.src, self.buf
+            for n, slot, half, to in ((0, 1, A, right), (3, 2, B, left), (1, 1, B, right), (2, 2, A, left)):
+                send(src.at[half], buf.at[slot, half], self.s.at[n], self.r.at[n], to, self.when)
+
+        def wait(self, slot, half, n):
+            arrived(self.buf.at[slot, half], self.s.at[n], self.r.at[n], self.when)
+
+        def middle(self):
+            buf = self.buf
+            self.wait(1, A, 0)
+            send(buf.at[1, A], buf.at[3, A], self.s.at[4], self.r.at[4], right, self.when)
+            self.wait(2, B, 3)
+            send(buf.at[2, B], buf.at[3, B], self.s.at[5], self.r.at[5], left, self.when)
+            self.wait(1, B, 1)
+            self.wait(2, A, 2)
+
+        def end(self):
+            self.wait(3, A, 4)
+            self.wait(3, B, 5)
 
     def w_rows(step):
         s = lax.rem(hx + step + nhead, nhead)
         return pl.ds(pl.multiple_of(s * SH, SH), SH)
 
+    def project(buf, i):
+        total = None
+        for slot, step in ((0, 0), (1, -1), (2, 1)):
+            part = dot(buf[slot], W[i, w_rows(step), :])
+            total = part if total is None else total + part
+        ACC[i] = total
+
+    def projected(buf, i):
+        full = (ACC[i] + dot(buf[3], W[i, w_rows(2), :])).astype(BF16)
+        low, high = full[:, :HD], full[:, HD:]
+        return jnp.where(core == 0, low, high), jnp.where(core == 0, high, low)
+
+    pl.semaphore_wait(barrier, count)
+
+    mine = Gather(feat, F, xs, xr, None)
+    far = Gather(FF.at[0], FF, fs, fr, far_here)
+    mine.begin()
+    out_far = ((core == 1) & has[2]) | ((core == 0) & has[-2])
+    far_to = (lax.rem(chip + jnp.where(core == 1, 2, -2) + nchip, nchip) * 2 + oth, hx)
+    send(feat, FF.at[0], fs.at[6], fr.at[6], far_to, out_far)
+    send(BQ.at[core], BQ.at[core], bs.at[0], br.at[0], partner)
+    spread(DO, dout.at[:, own_col], dout.at[:, oth_col])
+
     load_f.wait()
     load_w.wait()
+    mine.middle()
+    arrived(FF.at[0], fs.at[6], fr.at[6], far_here)
+    far.begin()
     for i in range(3):
-        ACC[i] = dot(F[0], W[i, w_rows(0), :])
-    x_arrived(1, A, 0)
-    send(F.at[1, A], F.at[3, A], xs.at[4], xr.at[4], right)
-    x_arrived(2, B, 3)
-    send(F.at[2, B], F.at[3, B], xs.at[5], xr.at[5], left)
-    x_arrived(1, B, 1)
-    for i in range(3):
-        ACC[i] += dot(F[1], W[i, w_rows(-1), :])
-    x_arrived(2, A, 2)
-    for i in range(3):
-        ACC[i] += dot(F[2], W[i, w_rows(1), :])
+        project(F, i)
     relay(DO)
-    x_arrived(3, A, 4)
-    x_arrived(3, B, 5)
+    mine.end()
     for kind, i in ((K, 1), (V, 2), (Q, 0)):
-        full = (ACC[i] + dot(F[3], W[i, w_rows(2), :])).astype(BF16)
-        low, high = full[:, :HD], full[:, HD:]
-        WIN[kind, 3 + core] = jnp.where(core == 0, low, high)
-        OTH[kind] = jnp.where(core == 0, high, low)
+        WIN[kind, 3 + core], OTH[kind] = projected(F, i)
         spread(kind, WIN.at[kind, 3 + core], OTH.at[kind])
+    far.middle()
+
+    @pl.when(far_here)
+    def _():
+        for i in range(3):
+            project(FF, i)
 
     win_arrived(Q, 3 + oth)
     load_d.wait()
@@ -228,15 +300,23 @@
     win_arrived(V, 3 + oth)
     scores(3)
     scores(4)
-    relay(K)
-    relay(V)
-    scores(2)
-    scores(5)
-    relay(Q)
-    for s in (1, 6, 0, 7):
+    far.end()
+    for kind, i in ((K, 1), (V, 2), (Q, 0)):
+
+        @pl.when(far_here)
+        def _():
+            WIN[kind, far_slot], FO[kind] = projected(FF, i)
+
+        to_partner(kind, far_slot, FO.at[kind], 5, far_here)
+    for s in (2, 5, 1, 6):
         win_arrived(K, s)
         win_arrived(V, s)
         scores(s)
+    win_arrived(K, far_oth, far_there)
+    win_arrived(V, far_oth, far_there)
+    win_arrived(Q, far_oth, far_there)
+    scores(0)
+    scores(7)
 
     m = jnp.max(MX[...], axis=0, keepdims=True)
     step = 32
@@ -259,7 +339,7 @@
         first = 6 + PAD + 4 * d
         for half in range(2):
             STO[n, 4:8, half * SH : (half + 1) * SH] = BQ[half, first : first + 4, :]
-        send(STO.at[n], STI.at[3 - n], ss.at[n], sr.at[3 - n], at(d, core))
+        send(STO.at[n], STI.at[3 - n], ss.at[n], sr.at[3 - n], at(d, core), has[d])
 
     def weights(n, carry):
         rows = pl.ds(pl.multiple_of(n * step, step), step)
@@ -292,9 +372,10 @@
         n, half = SOURCE[s]
         if n not in seen:
             seen.add(n)
-            arrived(STI.at[n], ss.at[n], sr.at[n])
-        if s not in (2, 5):
+            arrived(STI.at[n], ss.at[n], sr.at[n], has[FAR[n]])
+        if s in (1, 6, 0, 7):
             win_arrived(DO, s)
+        if s in (1, 2, 5, 6):
             win_arrived(Q, s)
         cols = slice(half * SH, (half + 1) * SH)
         sm, sil, srd = (STI[n, i : i + 1, cols] for i in range(3))
@@ -350,8 +431,11 @@
     store.start()
     att_own.wait()
     arrived(att.at[:, oth_col], as_.at[0], ar.at[0])
-    for c in started:
-        c.wait_send()
+    for c, when in started:
+        if when is None:
+            c.wait_send()
+        else:
+            pl.when(when)(c.wait_send)
     store.wait()
 
 
@@ -361,6 +445,7 @@
     def body(features, w_qkv, block_links, d_out):
         w = jnp.transpose(w_qkv, (1, 0, 2))
         any_spec = pl.BlockSpec(memory_space=pl.ANY)
+        hbm_spec = pl.BlockSpec(memory_space=pltpu.HBM)
         dma = pltpu.SemaphoreType.DMA
         vmem = pltpu.VMEM
         return tuple(
@@ -370,12 +455,7 @@
                     jax.ShapeDtypeStruct((SH, SH), BF16),
                     jax.ShapeDtypeStruct((SH, SH), BF16),
                 ],
-                in_specs=[
-                    any_spec,
-                    any_spec,
-                    pl.BlockSpec(memory_space=pltpu.SMEM),
-                    any_spec,
-                ],
+                in_specs=[hbm_spec] * 4,
                 out_specs=[any_spec, any_spec],
                 scratch_shapes=[
                     vmem((4, SH, SH), BF16),
@@ -400,9 +480,14 @@
                     vmem((6, BLK, SH), BF16),
                     vmem((6, BLK, SH), BF16),
                     vmem((SH, SH), BF16),
-                    dma((5,)),
+                    vmem((4, SH, SH), BF16),
+                    vmem((4, SH, HD), BF16),
+                    pltpu.SMEM((2, 9), jnp.int32),
                     dma((6,)),
                     dma((6,)),
+                    dma((6,)),
+                    dma((7,)),
+                    dma((7,)),
                     dma((4, 7)),
                     dma((4, 8)),
                     dma((1,)),
@@ -419,7 +504,7 @@
                 compiler_params=pltpu.CompilerParams(
                     collective_id=0,
                     has_side_effects=True,
-                    vmem_limit_bytes=48 * 1024 * 1024,
+                    vmem_limit_bytes=60 * 1024 * 1024,
                 ),
             )(features, w, block_links, d_out)
         )

time: 64.1 us -> 52.2 us (0.81)
  the two profiles are of different devices: /device:TPU:1 before, /device:TPU:258 now
where the time goes in v2:
time: 52.2 us; the launch traced here: 52 us
  Pallas kernels  48.2 us (92%)
  local copies, waits for them, and re-layouts  3.14 us (6%)
  between operations  0.64 us (1%)
    pallas_call x1, Pallas kernels, body(): pl.pallas_call(functools.partial(kernel, nctx, nhead), out_shape=[jax.Sha...  48.2 us
    unnamed x2, local copies, waits for them, and re-layouts  3.14 us

profile of v2, /device:TPU:258, one launch (start us, length us, event | category | flops | bytes accessed | tf_op | source)
XLA Modules:
  0.0 52.0 jit_solution(8924165074858072730)
XLA Ops:
  0.6 48.2 %shard_map.59 = (bf16[256,256]{1,0:T(8,128)(2,1)}, bf16[256,256]{1,0:T(8,128)(2,1)}) custom-call(bf16[256,256]{1,0:T(8,128)(2,1)} %feat.1, bf16[3,1024,256]{2,1,0:T(8,128)(2,1)} %bitcast.1, s32[2,9]{1,0:T(2,128)} %links.1, bf16[256,256]{1,0:T(8,128)(2,1)} %dout.1), custom_call_target="tpu_custom_call" | custom-call | tf_op jit(solution)/shard_map/pallas_call | solution.py:452
  48.9 1.6 %copy.8 = bf16[256,256]{1,0:T(8,128)(2,1)} copy(bf16[256,256]{1,0:T(8,128)(2,1)} %get-tuple-element.4) | data formatting | bytes 262144
  50.4 1.6 %copy.9 = bf16[256,256]{1,0:T(8,128)(2,1)} copy(bf16[256,256]{1,0:T(8,128)(2,1)} %get-tuple-element.5) | data formatting | bytes 262144

commit v3 on v2

--- a/solution.py
+++ b/solution.py
@@ -11,6 +11,7 @@
 MESH = pl.DeviceIdType.MESH
 BLK = 128
 HD = 128
+HALF = 64
 SH = 256
 SCALE = HD ** (-0.5)
 C2 = SCALE * math.log2(math.e)
@@ -20,6 +21,8 @@
 DO, K, V, Q = range(4)
 PAD = 2
 ROWS = 24
+PAIRS = ((3, 4), (0, 7), (2, 5), (1, 6))
+ORDER = (0, 2, 1, 3)
 FAR = (-2, -1, 1, 2)
 SOURCE = {0: (0, 1), 1: (1, 0), 2: (1, 1), 5: (2, 0), 6: (2, 1), 7: (3, 0)}
 
@@ -55,12 +58,15 @@
     DP,
     PB,
     DSB,
+    PK,
+    TK,
+    KS,
+    KDP,
+    MS,
     KT,
     VT,
-    MX,
     STO,
     STI,
-    DKV,
     AST,
     GP,
     GST,
@@ -216,10 +222,12 @@
         def wait(self, slot, half, n):
             arrived(self.buf.at[slot, half], self.s.at[n], self.r.at[n], self.when)
 
-        def middle(self):
+        def pass_right(self):
             buf = self.buf
-            self.wait(1, A, 0)
             send(buf.at[1, A], buf.at[3, A], self.s.at[4], self.r.at[4], right, self.when)
+
+        def rest(self):
+            buf = self.buf
             self.wait(2, B, 3)
             send(buf.at[2, B], buf.at[3, B], self.s.at[5], self.r.at[5], left, self.when)
             self.wait(1, B, 1)
@@ -254,52 +262,97 @@
     far_to = (lax.rem(chip + jnp.where(core == 1, 2, -2) + nchip, nchip) * 2 + oth, hx)
     send(feat, FF.at[0], fs.at[6], fr.at[6], far_to, out_far)
     send(BQ.at[core], BQ.at[core], bs.at[0], br.at[0], partner)
-    spread(DO, dout.at[:, own_col], dout.at[:, oth_col])
-
+    for tab in (PB, DSB):
+        tab[:SH, SH:] = jnp.zeros((SH, SH), BF16)
+        tab[7 * SH :, :SH] = jnp.zeros((SH, SH), BF16)
+    for tab in (PK, TK):
+        for pos, e in enumerate(ORDER):
+            where = slice(7 * SH, 8 * SH) if e < 2 else slice(0, SH)
+            tab[pos * BLK : (pos + 1) * BLK, where] = jnp.zeros((BLK, SH), BF16)
     load_f.wait()
     load_w.wait()
-    mine.middle()
+    mine.wait(1, A, 0)
+    mine.pass_right()
+    spread(DO, dout.at[:, own_col], dout.at[:, oth_col])
+    mine.rest()
+    for i in range(3):
+        project(F, i)
+    mine.end()
     arrived(FF.at[0], fs.at[6], fr.at[6], far_here)
     far.begin()
-    for i in range(3):
-        project(F, i)
-    relay(DO)
-    mine.end()
     for kind, i in ((K, 1), (V, 2), (Q, 0)):
         WIN[kind, 3 + core], OTH[kind] = projected(F, i)
         spread(kind, WIN.at[kind, 3 + core], OTH.at[kind])
-    far.middle()
+    relay(DO)
+
+    win_arrived(Q, 3 + oth)
+    load_d.wait()
+    win_arrived(DO, 3 + oth)
+    arrived(BQ.at[oth], bs.at[0], br.at[0])
+
+    def lanes(s):
+        return {0: (0,), 7: (1,)}.get(s, (0, 1))
+
+    def scores(pair):
+        tops = [None, None]
+        for s in pair:
+            for half in lanes(s):
+                cols = slice(half * SH, (half + 1) * SH)
+                x = dot_t(WIN[K, s], WIN[Q, 3 + half]) * C2
+                for b in range(2):
+                    wb = 2 * s + b + PAD
+                    y = x[b * BLK : (b + 1) * BLK] + BQ[half, wb : wb + 1, :]
+                    S[s * SH + b * BLK : s * SH + (b + 1) * BLK, cols] = y
+                    top = fold8(y, jnp.max)
+                    tops[half] = top if tops[half] is None else jnp.maximum(tops[half], top)
+                DP[s * SH : (s + 1) * SH, cols] = dot_t(WIN[V, s], WIN[DO, 3 + half])
+        return jnp.max(jnp.concatenate(tops, axis=1), axis=0, keepdims=True)
+
+    def query_side(n, pair, m_old, l8, r8):
+        m_new = jnp.maximum(m_old, scores(pair))
+        MS[n] = m_new
+        shrink = jnp.exp2(m_old - m_new)
+        l8, r8 = l8 * shrink, r8 * shrink
+        for s in pair:
+            halves = lanes(s)
+            cols = slice(halves[0] * SH, (halves[-1] + 1) * SH)
+            step = 64 // len(halves)
+            top = m_new[:, cols]
+
+            def piece(i, carry):
+                l, r = carry
+                rows = pl.ds(pl.multiple_of(s * SH + i * step, step), step)
+                e = jnp.exp2(S[rows, cols] - top)
+                S[rows, cols] = e
+                return l + fold8(e, jnp.sum), r + fold8(e * DP[rows, cols], jnp.sum)
+
+            zero = jnp.zeros((8, SH * len(halves)), F32)
+            l, r = lax.fori_loop(0, SH // step, piece, (zero, zero))
+            if len(halves) == 1:
+                pads = [jnp.zeros((8, SH), F32)] * 2
+                pads[halves[0]] = l
+                l = jnp.concatenate(pads, axis=1)
+                pads[halves[0]] = r
+                r = jnp.concatenate(pads, axis=1)
+            l8, r8 = l8 + l, r8 + r
+        return m_new, l8, r8
+
+    win_arrived(K, 3 + oth)
+    win_arrived(V, 3 + oth)
+    m = jnp.full((1, 2 * SH), -3e38, F32)
+    l8 = jnp.zeros((8, 2 * SH), F32)
+    r8 = l8
+    m, l8, r8 = query_side(0, PAIRS[0], m, l8, r8)
+
+    far.wait(1, A, 0)
+    far.pass_right()
+    far.rest()
 
     @pl.when(far_here)
     def _():
         for i in range(3):
             project(FF, i)
 
-    win_arrived(Q, 3 + oth)
-    load_d.wait()
-    win_arrived(DO, 3 + oth)
-    arrived(BQ.at[oth], bs.at[0], br.at[0])
-    MX[...] = jnp.full(MX.shape, -3e38, F32)
-
-    def scores(s):
-        for b in range(2):
-            wb = 2 * s + b
-            kb = WIN[K, s, b * BLK : (b + 1) * BLK, :]
-            vb = WIN[V, s, b * BLK : (b + 1) * BLK, :]
-            rows = slice(wb * BLK, (wb + 1) * BLK)
-            for half in range(2):
-                cols = slice(half * SH, (half + 1) * SH)
-                x = dot_t(kb, WIN[Q, 3 + half]) * C2 + BQ[half, wb + PAD : wb + PAD + 1, :]
-                S[rows, cols] = x
-                MX[:, cols] = jnp.maximum(MX[:, cols], fold8(x, jnp.max))
-                DP[rows, cols] = dot_t(vb, WIN[DO, 3 + half])
-        KT[:, s * SH : (s + 1) * SH] = WIN[K, s].T
-        VT[:, s * SH : (s + 1) * SH] = WIN[V, s].T
-
-    win_arrived(K, 3 + oth)
-    win_arrived(V, 3 + oth)
-    scores(3)
-    scores(4)
     far.end()
     for kind, i in ((K, 1), (V, 2), (Q, 0)):
 
@@ -308,30 +361,19 @@
             WIN[kind, far_slot], FO[kind] = projected(FF, i)
 
         to_partner(kind, far_slot, FO.at[kind], 5, far_here)
-    for s in (2, 5, 1, 6):
-        win_arrived(K, s)
-        win_arrived(V, s)
-        scores(s)
-    win_arrived(K, far_oth, far_there)
-    win_arrived(V, far_oth, far_there)
-    win_arrived(Q, far_oth, far_there)
-    scores(0)
-    scores(7)
-
-    m = jnp.max(MX[...], axis=0, keepdims=True)
-    step = 32
-
-    def totals(n, carry):
-        l, rd = carry
-        rows = pl.ds(pl.multiple_of(n * step, step), step)
-        e = jnp.exp2(S[rows, :] - m)
-        S[rows, :] = e
-        return l + fold8(e, jnp.sum), rd + fold8(e * DP[rows, :], jnp.sum)
-
-    zero = jnp.zeros((8, 2 * SH), F32)
-    l, rd = lax.fori_loop(0, 8 * SH // step, totals, (zero, zero))
-    il = 1.0 / jnp.sum(l, axis=0, keepdims=True)
-    rd = jnp.sum(rd, axis=0, keepdims=True) * il
+    for kind in (K, V):
+        win_arrived(kind, far_oth, far_there)
+    for n, pair in enumerate(PAIRS):
+        if n == 0:
+            continue
+        if n > 1:
+            for s in pair:
+                win_arrived(K, s)
+                win_arrived(V, s)
+        m, l8, r8 = query_side(n, pair, m, l8, r8)
+
+    il = 1.0 / jnp.sum(l8, axis=0, keepdims=True)
+    rd = jnp.sum(r8, axis=0, keepdims=True) * il
     for n, d in enumerate(FAR):
         STO[n, 0:1, :] = m
         STO[n, 1:2, :] = il
@@ -341,14 +383,25 @@
             STO[n, 4:8, half * SH : (half + 1) * SH] = BQ[half, first : first + 4, :]
         send(STO.at[n], STI.at[3 - n], ss.at[n], sr.at[3 - n], at(d, core), has[d])
 
-    def weights(n, carry):
-        rows = pl.ds(pl.multiple_of(n * step, step), step)
-        p = S[rows, :] * il
-        PB[rows, :] = p.astype(BF16)
-        DSB[rows, :] = (p * (DP[rows, :] - rd)).astype(BF16)
-        return carry
-
-    lax.fori_loop(0, 8 * SH // step, weights, 0)
+    for n, pair in enumerate(PAIRS):
+        factor = jnp.exp2(MS[n] - m) * il
+        for s in pair:
+            halves = lanes(s)
+            cols = slice(halves[0] * SH, (halves[-1] + 1) * SH)
+            step = 64 // len(halves)
+            f, r0 = factor[:, cols], rd[:, cols]
+
+            def piece(i, carry):
+                rows = pl.ds(pl.multiple_of(s * SH + i * step, step), step)
+                p = S[rows, cols] * f
+                PB[rows, cols] = p.astype(BF16)
+                DSB[rows, cols] = (p * (DP[rows, cols] - r0)).astype(BF16)
+                return carry
+
+            lax.fori_loop(0, SH // step, piece, 0)
+    for s in range(8):
+        KT[:, s * SH : (s + 1) * SH] = WIN[K, s].T
+        VT[:, s * SH : (s + 1) * SH] = WIN[V, s].T
     out = dot(VT[...], PB[...]).T.astype(BF16)
     AST[0] = out[:SH]
     AST[1] = out[SH:]
@@ -356,77 +409,100 @@
     att_own = pltpu.make_async_copy(AST.at[core], att.at[:, own_col], loc.at[3])
     att_own.start()
 
-    def hand_over(i, low, high):
-        GP[i, :, own_col] = jnp.where(core == 0, low, high)
-        GST[i] = jnp.where(core == 0, high, low)
-        send(GST.at[i], GP.at[i, :, own_col], gs.at[i], gr.at[i], partner)
+    def hand_over(i, n, low, high):
+        rows = pl.ds(n * BLK, BLK)
+        GP[i, rows, own_col] = jnp.where(core == 0, low, high)
+        GST[i, rows] = jnp.where(core == 0, high, low)
+        send(GST.at[i, rows], GP.at[i, rows, own_col], gs.at[i, n], gr.at[i, n], partner)
 
     dq = (dot(KT[...], DSB[...]) * SCALE).T.astype(BF16)
-    hand_over(0, dq[:SH], dq[SH:])
-
-    own = slice(3 * SH, 5 * SH)
-    DKV[0] = dot(DSB[own, :], WIN[Q, 3:5].reshape(2 * SH, HD))
-    DKV[1] = dot(PB[own, :], WIN[DO, 3:5].reshape(2 * SH, HD))
-    seen = set()
-    for s in (2, 5, 1, 6, 0, 7):
-        n, half = SOURCE[s]
-        if n not in seen:
-            seen.add(n)
-            arrived(STI.at[n], ss.at[n], sr.at[n], has[FAR[n]])
+    for n in range(2):
+        rows = slice(n * BLK, (n + 1) * BLK)
+        hand_over(0, n, dq[rows], dq[SH:][rows])
+
+    for pos, e in enumerate(ORDER):
+        rows, keys = slice(pos * BLK, (pos + 1) * BLK), slice((6 + e) * BLK, (7 + e) * BLK)
+        PK[rows, 3 * SH : 5 * SH] = PB[keys, :]
+        TK[rows, 3 * SH : 5 * SH] = DSB[keys, :]
+
+    def spans(s):
+        return {0: (0,), 7: (1,)}.get(s, (0, 1))
+
+    win_arrived(Q, far_oth, far_there)
+    for s in (0, 7, 2, 5, 1, 6):
         if s in (1, 6, 0, 7):
             win_arrived(DO, s)
         if s in (1, 2, 5, 6):
             win_arrived(Q, s)
-        cols = slice(half * SH, (half + 1) * SH)
-        sm, sil, srd = (STI[n, i : i + 1, cols] for i in range(3))
-        qs, ds = WIN[Q, s], WIN[DO, s]
-        for e in range(4):
-            rows = slice((e % 2) * BLK, (e % 2 + 1) * BLK)
-            x = dot_t(WIN[K, 3 + e // 2, rows, :], qs) * C2 + STI[n, 4 + e : 5 + e, cols]
-            p = jnp.exp2(x - sm) * sil
-            t = p * (dot_t(WIN[V, 3 + e // 2, rows, :], ds) - srd)
-            rows = slice(e * BLK, (e + 1) * BLK)
-            DKV[0, rows, :] += dot(t.astype(BF16), qs)
-            DKV[1, rows, :] += dot(p.astype(BF16), ds)
-    dk = (DKV[0] * SCALE).astype(BF16)
-    hand_over(1, dk[:SH], dk[SH:])
-    dv = DKV[1].astype(BF16)
-    hand_over(2, dv[:SH], dv[SH:])
-
-    for i in range(3):
-        arrived(GP.at[i, :, oth_col], gs.at[i], gr.at[i])
-
-    def partial(step):
+        for c in spans(s):
+            rows = slice(c * SH, (c + 1) * SH)
+            KS[s, rows] = dot_t(WIN[K, 3 + c], WIN[Q, s]) * C2
+            KDP[s, rows] = dot_t(WIN[V, 3 + c], WIN[DO, s])
+    for n, d in enumerate(FAR):
+        arrived(STI.at[n], ss.at[n], sr.at[n], has[d])
+    wide = (8 * SH, HD)
+    for part in range(2):
+        for s in (2, 5, 1, 6, 0, 7):
+            n, half = SOURCE[s]
+            cols = slice(half * SH, (half + 1) * SH)
+            sm, sil, srd = (STI[n, i : i + 1, cols] for i in range(3))
+            for c in spans(s):
+                e = 2 * c + part
+                pos = 2 * part + c
+                shift = STI[n, 4 + e : 5 + e, cols] - sm
+
+                def piece(i, carry):
+                    src = pl.ds(pl.multiple_of(e * BLK + i * 64, 64), 64)
+                    dst = pl.ds(pl.multiple_of(pos * BLK + i * 64, 64), 64)
+                    p = jnp.exp2(KS[s, src] + shift) * sil
+                    PK[dst, s * SH : (s + 1) * SH] = p.astype(BF16)
+                    TK[dst, s * SH : (s + 1) * SH] = (p * (KDP[s, src] - srd)).astype(BF16)
+                    return carry
+
+                lax.fori_loop(0, BLK // 64, piece, 0)
+        rows = slice(part * SH, (part + 1) * SH)
+        dk = (dot(TK[rows, :], WIN[Q].reshape(wide)) * SCALE).astype(BF16)
+        hand_over(1, part, dk[:BLK], dk[BLK:])
+        dv = dot(PK[rows, :], WIN[DO].reshape(wide)).astype(BF16)
+        hand_over(2, part, dv[:BLK], dv[BLK:])
+
+    def partial(part, step):
         rows = w_rows(step)
-        return sum(dot_t(GP[i], W[i, rows, :]) for i in range(3))
-
-    def pass_on(n, to):
-        send(RSO.at[n], RSI.at[n], rs.at[n], rr.at[n], to)
-
-    def rs_arrived(n):
-        arrived(RSI.at[n], rs.at[n], rr.at[n])
-        return RSI[n].astype(F32)
-
-    gx = partial(2)
-    RSO[0] = gx[:BLK].astype(BF16)
-    pass_on(0, right)
-    RSO[1] = gx[BLK:].astype(BF16)
-    pass_on(1, left)
-    g_r = partial(1)
-    RSO[2] = g_r[BLK:].astype(BF16)
-    pass_on(2, right)
-    g_l = partial(-1)
-    RSO[3] = g_l[:BLK].astype(BF16)
-    pass_on(3, left)
-    RSO[4] = (g_r[:BLK] + rs_arrived(0)).astype(BF16)
-    pass_on(4, right)
-    RSO[5] = (g_l[BLK:] + rs_arrived(1)).astype(BF16)
-    pass_on(5, left)
-    g_o = partial(0)
-    g_a = g_o[:BLK] + rs_arrived(3)
-    g_b = g_o[BLK:] + rs_arrived(2)
-    OUT[:BLK] = (g_a + rs_arrived(4)).astype(BF16)
-    OUT[BLK:] = (g_b + rs_arrived(5)).astype(BF16)
+        mine = slice(part * BLK, (part + 1) * BLK)
+        return sum(dot_t(GP[i, mine, :], W[i, rows, :]) for i in range(3))
+
+    def pass_on(part, n, value, to):
+        RSO[part, n] = value.astype(BF16)
+        send(RSO.at[part, n], RSI.at[part, n], rs.at[part, n], rr.at[part, n], to)
+
+    def rs_arrived(part, n):
+        arrived(RSI.at[part, n], rs.at[part, n], rr.at[part, n])
+        return RSI[part, n].astype(F32)
+
+    kept = []
+    for part in range(2):
+        for i in range(3):
+            rows = pl.ds(part * BLK, BLK)
+            arrived(GP.at[i, rows, oth_col], gs.at[i, part], gr.at[i, part])
+        gx = partial(part, 2)
+        pass_on(part, 0, gx[:HALF], right)
+        pass_on(part, 1, gx[HALF:], left)
+        g_r = partial(part, 1)
+        pass_on(part, 2, g_r[HALF:], right)
+        g_l = partial(part, -1)
+        pass_on(part, 3, g_l[:HALF], left)
+        kept.append((g_r[:HALF], g_l[HALF:]))
+    for part in range(2):
+        g_r, g_l = kept[part]
+        pass_on(part, 4, g_r + rs_arrived(part, 0), right)
+        pass_on(part, 5, g_l + rs_arrived(part, 1), left)
+    for part in range(2):
+        g_o = partial(part, 0)
+        g_a = g_o[:HALF] + rs_arrived(part, 3)
+        g_b = g_o[HALF:] + rs_arrived(part, 2)
+        start = part * BLK
+        OUT[start : start + HALF] = (g_a + rs_arrived(part, 4)).astype(BF16)
+        OUT[start + HALF : start + BLK] = (g_b + rs_arrived(part, 5)).astype(BF16)
     store = pltpu.make_async_copy(OUT, gout, loc.at[4])
     store.start()
     att_own.wait()
@@ -468,17 +544,20 @@
                     vmem((8 * SH, 2 * SH), F32),
                     vmem((8 * SH, 2 * SH), BF16),
                     vmem((8 * SH, 2 * SH), BF16),
+                    vmem((2 * SH, 8 * SH), BF16),
+                    vmem((2 * SH, 8 * SH), BF16),
+                    vmem((8, 2 * SH, SH), F32),
+                    vmem((8, 2 * SH, SH), F32),
+                    vmem((4, 1, 2 * SH), F32),
                     vmem((HD, 8 * SH), BF16),
                     vmem((HD, 8 * SH), BF16),
-                    vmem((8, 2 * SH), F32),
                     vmem((4, 8, 2 * SH), F32),
                     vmem((4, 8, 2 * SH), F32),
-                    vmem((2, 2 * SH, HD), F32),
                     vmem((2, SH, HD), BF16),
                     vmem((3, SH, SH), BF16),
                     vmem((3, SH, HD), BF16),
-                    vmem((6, BLK, SH), BF16),
-                    vmem((6, BLK, SH), BF16),
+                    vmem((2, 6, HALF, SH), BF16),
+                    vmem((2, 6, HALF, SH), BF16),
                     vmem((SH, SH), BF16),
                     vmem((4, SH, SH), BF16),
                     vmem((4, SH, HD), BF16),
@@ -496,10 +575,10 @@
                     dma((4,)),
                     dma((1,)),
                     dma((1,)),
-                    dma((3,)),
-                    dma((3,)),
-                    dma((6,)),
-                    dma((6,)),
+                    dma((3, 2)),
+                    dma((3, 2)),
+                    dma((2, 6)),
+                    dma((2, 6)),
                 ],
                 compiler_params=pltpu.CompilerParams(
                     collective_id=0,

time: 52.2 us -> 46.1 us (0.88)
  the two profiles are of different devices: /device:TPU:258 before, /device:TPU:1 now
where the time goes in v3:
time: 46.1 us; the launch traced here: 45.5 us
  Pallas kernels  41.7 us (90%)
  local copies, waits for them, and re-layouts  3.14 us (7%)
  between operations  0.64 us (1%)
    pallas_call x1, Pallas kernels, body(): pl.pallas_call(functools.partial(kernel, nctx, nhead), out_shape=[jax.Sha...  41.7 us
    unnamed x2, local copies, waits for them, and re-layouts  3.14 us

profile of v3, /device:TPU:1, one launch (start us, length us, event | category | flops | bytes accessed | tf_op | source)
XLA Modules:
  0.0 45.5 jit_solution(2907300389566827744)
XLA Ops:
  0.6 41.7 %shard_map.59 = (bf16[256,256]{1,0:T(8,128)(2,1)}, bf16[256,256]{1,0:T(8,128)(2,1)}) custom-call(bf16[256,256]{1,0:T(8,128)(2,1)} %feat.1, bf16[3,1024,256]{2,1,0:T(8,128)(2,1)} %bitcast.1, s32[2,9]{1,0:T(2,128)} %links.1, bf16[256,256]{1,0:T(8,128)(2,1)} %dout.1), custom_call_target="tpu_custom_call" | custom-call | tf_op jit(solution)/shard_map/pallas_call | solution.py:528
  42.4 1.6 %copy.8 = bf16[256,256]{1,0:T(8,128)(2,1)} copy(bf16[256,256]{1,0:T(8,128)(2,1)} %get-tuple-element.4) | data formatting | bytes 262144
  43.9 1.6 %copy.9 = bf16[256,256]{1,0:T(8,128)(2,1)} copy(bf16[256,256]{1,0:T(8,128)(2,1)} %get-tuple-element.5) | data formatting | bytes 262144

commit v4 on v3

--- a/solution.py
+++ b/solution.py
@@ -46,8 +46,7 @@
     w,
     links,
     dout,
-    att,
-    gout,
+    both,
     F,
     W,
     ACC,
@@ -115,6 +114,7 @@
     oth_col = pl.ds(pl.multiple_of(oth * HD, HD), HD)
     A, B = pl.ds(0, BLK), pl.ds(BLK, BLK)
 
+    att, gout = both.at[0], both.at[1]
     load_l = pltpu.make_async_copy(links, LK, loc.at[5])
     load_l.start()
     barrier = pltpu.get_barrier_semaphore()
@@ -190,52 +190,71 @@
 
     near = {0: has[-2], 1: has[-1], 2: has[-1], 5: has[1], 6: has[1], 7: has[2]}
 
-    def win_arrived(kind, slot, when=None):
-        if isinstance(slot, int):
-            when = near[slot]
-        arrived(WIN.at[kind, slot], ws.at[kind, 0], wr.at[kind, slot], when)
-
-    def to_partner(kind, slot, src, n, when=None):
-        send(src, WIN.at[kind, slot], ws.at[kind, n], wr.at[kind, slot], partner, when)
-
-    def spread(kind, own, other):
-        to_partner(kind, 3 + core, other, 0)
+    def do_arrived(slot):
+        when = near[slot] if isinstance(slot, int) else None
+        arrived(WIN.at[DO, slot], ws.at[DO, 0], wr.at[DO, slot], when)
+
+    KV, QQ = pl.ds(K, 2), pl.ds(Q, 1)
+
+    def kvq_arrived(kinds, slot):
+        kind = kinds.start
+        arrived(WIN.at[kinds, slot], ws.at[kind, 0], wr.at[kind, slot], near[slot])
+
+    def partner_arrived(kinds):
+        kind = kinds.start
+        arrived(WIN.at[kinds, 3 + oth], ws.at[kind, 0], wr.at[kind, 3 + oth])
+
+    def spread_do():
+        own, other = dout.at[:, own_col], dout.at[:, oth_col]
         for n, (d, slot) in enumerate(((1, 1 + core), (-1, 5 + core))):
-            send(own, WIN.at[kind, slot], ws.at[kind, 1 + 2 * n], wr.at[kind, slot], at(d, core), has[d])
-            send(other, WIN.at[kind, slot], ws.at[kind, 2 + 2 * n], wr.at[kind, slot], at(d, oth), has[d])
-
-    def relay(kind):
+            dst, r_sem = WIN.at[DO, slot], wr.at[DO, slot]
+            send(own, dst, ws.at[DO, 1 + 2 * n], r_sem, at(d, core), has[d])
+            send(other, dst, ws.at[DO, 2 + 2 * n], r_sem, at(d, oth), has[d])
+
+    def spread(kinds):
+        kind = kinds.start
+        send(OTH.at[kinds], WIN.at[kinds, 3 + core], ws.at[kind, 0], wr.at[kind, 3 + core], partner)
+        for n, (d, slot) in enumerate(((1, 1 + core), (-1, 5 + core))):
+            for m, (src, to) in enumerate(((WIN.at[kinds, 3 + core], core), (OTH.at[kinds], oth))):
+                send(src, WIN.at[kinds, slot], ws.at[kind, 1 + 2 * n + m], wr.at[kind, slot], at(d, to), has[d])
+
+    def relay_do():
         for n, (d, slot, to) in enumerate(((1, 2, 0), (-1, 5, 7))):
-            win_arrived(kind, slot)
+            do_arrived(slot)
             both = has[1] & has[-1]
-            send(WIN.at[kind, slot], WIN.at[kind, to], ws.at[kind, 5 + n], wr.at[kind, to], at(d, core), both)
+            send(WIN.at[DO, slot], WIN.at[DO, to], ws.at[DO, 5 + n], wr.at[DO, to], at(d, core), both)
 
     class Gather:
         def __init__(self, src, buf, s, r, when):
             self.src, self.buf, self.s, self.r, self.when = src, buf, s, r, when
+            half = buf.shape[1] // 2
+            self.low, self.high = pl.ds(0, half), pl.ds(half, half)
 
         def begin(self):
-            src, buf = self.src, self.buf
-            for n, slot, half, to in ((0, 1, A, right), (3, 2, B, left), (1, 1, B, right), (2, 2, A, left)):
+            src, buf, low, high = self.src, self.buf, self.low, self.high
+            for n, slot, half, to in ((0, 1, low, right), (3, 2, high, left), (1, 1, high, right), (2, 2, low, left)):
                 send(src.at[half], buf.at[slot, half], self.s.at[n], self.r.at[n], to, self.when)
 
         def wait(self, slot, half, n):
             arrived(self.buf.at[slot, half], self.s.at[n], self.r.at[n], self.when)
 
         def pass_right(self):
-            buf = self.buf
-            send(buf.at[1, A], buf.at[3, A], self.s.at[4], self.r.at[4], right, self.when)
+            buf, low = self.buf, self.low
+            self.wait(1, low, 0)
+            send(buf.at[1, low], buf.at[3, low], self.s.at[4], self.r.at[4], right, self.when)
+
+        def pass_left(self):
+            buf, high = self.buf, self.high
+            self.wait(2, high, 3)
+            send(buf.at[2, high], buf.at[3, high], self.s.at[5], self.r.at[5], left, self.when)
 
         def rest(self):
-            buf = self.buf
-            self.wait(2, B, 3)
-            send(buf.at[2, B], buf.at[3, B], self.s.at[5], self.r.at[5], left, self.when)
-            self.wait(1, B, 1)
-            self.wait(2, A, 2)
+            self.wait(1, self.high, 1)
+            self.wait(2, self.low, 2)
 
         def end(self):
-            self.wait(3, A, 4)
-            self.wait(3, B, 5)
+            self.wait(3, self.low, 4)
+            self.wait(3, self.high, 5)
 
     def w_rows(step):
         s = lax.rem(hx + step + nhead, nhead)
@@ -246,10 +265,10 @@
         for slot, step in ((0, 0), (1, -1), (2, 1)):
             part = dot(buf[slot], W[i, w_rows(step), :])
             total = part if total is None else total + part
-        ACC[i] = total
+        ACC[i, : buf.shape[1]] = total
 
     def projected(buf, i):
-        full = (ACC[i] + dot(buf[3], W[i, w_rows(2), :])).astype(BF16)
+        full = (ACC[i, : buf.shape[1]] + dot(buf[3], W[i, w_rows(2), :])).astype(BF16)
         low, high = full[:, :HD], full[:, HD:]
         return jnp.where(core == 0, low, high), jnp.where(core == 0, high, low)
 
@@ -258,10 +277,10 @@
     mine = Gather(feat, F, xs, xr, None)
     far = Gather(FF.at[0], FF, fs, fr, far_here)
     mine.begin()
-    out_far = ((core == 1) & has[2]) | ((core == 0) & has[-2])
-    far_to = (lax.rem(chip + jnp.where(core == 1, 2, -2) + nchip, nchip) * 2 + oth, hx)
-    send(feat, FF.at[0], fs.at[6], fr.at[6], far_to, out_far)
+    out_two = ((core == 1) & has[2]) | ((core == 0) & has[-2])
+    send(feat, FF.at[0], fs.at[6], fr.at[6], at(jnp.where(core == 1, 2, -2), oth), out_two)
     send(BQ.at[core], BQ.at[core], bs.at[0], br.at[0], partner)
+    send(dout.at[:, oth_col], WIN.at[DO, 3 + core], ws.at[DO, 0], wr.at[DO, 3 + core], partner)
     for tab in (PB, DSB):
         tab[:SH, SH:] = jnp.zeros((SH, SH), BF16)
         tab[7 * SH :, :SH] = jnp.zeros((SH, SH), BF16)
@@ -271,23 +290,28 @@
             tab[pos * BLK : (pos + 1) * BLK, where] = jnp.zeros((BLK, SH), BF16)
     load_f.wait()
     load_w.wait()
-    mine.wait(1, A, 0)
     mine.pass_right()
-    spread(DO, dout.at[:, own_col], dout.at[:, oth_col])
+    spread_do()
+    mine.pass_left()
+    arrived(FF.at[0], fs.at[6], fr.at[6], far_here)
+    far.begin()
     mine.rest()
     for i in range(3):
         project(F, i)
     mine.end()
-    arrived(FF.at[0], fs.at[6], fr.at[6], far_here)
-    far.begin()
-    for kind, i in ((K, 1), (V, 2), (Q, 0)):
-        WIN[kind, 3 + core], OTH[kind] = projected(F, i)
-        spread(kind, WIN.at[kind, 3 + core], OTH.at[kind])
-    relay(DO)
-
-    win_arrived(Q, 3 + oth)
+    WIN[K, 3 + core], OTH[K] = projected(F, 1)
+    WIN[V, 3 + core], OTH[V] = projected(F, 2)
+    spread(KV)
+    WIN[Q, 3 + core], OTH[Q] = projected(F, 0)
+    early = len(started)
+    spread(QQ)
+    far.pass_right()
+    far.pass_left()
+    relay_do()
+
+    partner_arrived(QQ)
     load_d.wait()
-    win_arrived(DO, 3 + oth)
+    do_arrived(3 + oth)
     arrived(BQ.at[oth], bs.at[0], br.at[0])
 
     def lanes(s):
@@ -327,7 +351,7 @@
                 return l + fold8(e, jnp.sum), r + fold8(e * DP[rows, cols], jnp.sum)
 
             zero = jnp.zeros((8, SH * len(halves)), F32)
-            l, r = lax.fori_loop(0, SH // step, piece, (zero, zero))
+            l, r = lax.fori_loop(0, SH // step, piece, (zero, zero), unroll=2)
             if len(halves) == 1:
                 pads = [jnp.zeros((8, SH), F32)] * 2
                 pads[halves[0]] = l
@@ -337,15 +361,12 @@
             l8, r8 = l8 + l, r8 + r
         return m_new, l8, r8
 
-    win_arrived(K, 3 + oth)
-    win_arrived(V, 3 + oth)
+    partner_arrived(KV)
     m = jnp.full((1, 2 * SH), -3e38, F32)
     l8 = jnp.zeros((8, 2 * SH), F32)
     r8 = l8
     m, l8, r8 = query_side(0, PAIRS[0], m, l8, r8)
 
-    far.wait(1, A, 0)
-    far.pass_right()
     far.rest()
 
     @pl.when(far_here)
@@ -354,23 +375,20 @@
             project(FF, i)
 
     far.end()
-    for kind, i in ((K, 1), (V, 2), (Q, 0)):
-
-        @pl.when(far_here)
-        def _():
-            WIN[kind, far_slot], FO[kind] = projected(FF, i)
-
-        to_partner(kind, far_slot, FO.at[kind], 5, far_here)
-    for kind in (K, V):
-        win_arrived(kind, far_oth, far_there)
-    for n, pair in enumerate(PAIRS):
-        if n == 0:
-            continue
-        if n > 1:
-            for s in pair:
-                win_arrived(K, s)
-                win_arrived(V, s)
-        m, l8, r8 = query_side(n, pair, m, l8, r8)
+
+    @pl.when(far_here)
+    def _():
+        for kind, i in ((K, 1), (V, 2), (Q, 0)):
+            WIN[kind, far_slot], FO[kind - 1] = projected(FF, i)
+
+    kvq = pl.ds(K, 3)
+    send(FO, WIN.at[kvq, far_slot], fs.at[7], fr.at[7], partner, far_here)
+    arrived(WIN.at[kvq, far_oth], fs.at[7], fr.at[7], far_there)
+    m, l8, r8 = query_side(1, PAIRS[1], m, l8, r8)
+    for n in (2, 3):
+        for s in PAIRS[n]:
+            kvq_arrived(KV, s)
+        m, l8, r8 = query_side(n, PAIRS[n], m, l8, r8)
 
     il = 1.0 / jnp.sum(l8, axis=0, keepdims=True)
     rd = jnp.sum(r8, axis=0, keepdims=True) * il
@@ -398,7 +416,7 @@
                 DSB[rows, cols] = (p * (DP[rows, cols] - r0)).astype(BF16)
                 return carry
 
-            lax.fori_loop(0, SH // step, piece, 0)
+            lax.fori_loop(0, SH // step, piece, 0, unroll=2)
     for s in range(8):
         KT[:, s * SH : (s + 1) * SH] = WIN[K, s].T
         VT[:, s * SH : (s + 1) * SH] = WIN[V, s].T
@@ -409,16 +427,17 @@
     att_own = pltpu.make_async_copy(AST.at[core], att.at[:, own_col], loc.at[3])
     att_own.start()
 
-    def hand_over(i, n, low, high):
-        rows = pl.ds(n * BLK, BLK)
+    def hand_over(i, rows, low, high):
         GP[i, rows, own_col] = jnp.where(core == 0, low, high)
         GST[i, rows] = jnp.where(core == 0, high, low)
-        send(GST.at[i, rows], GP.at[i, rows, own_col], gs.at[i, n], gr.at[i, n], partner)
+
+    def hand_on(kinds, n, rows):
+        send(GST.at[kinds, rows], GP.at[kinds, rows, own_col], gs.at[n], gr.at[n], partner)
 
     dq = (dot(KT[...], DSB[...]) * SCALE).T.astype(BF16)
-    for n in range(2):
-        rows = slice(n * BLK, (n + 1) * BLK)
-        hand_over(0, n, dq[rows], dq[SH:][rows])
+    every = pl.ds(0, SH)
+    hand_over(0, every, dq[:SH], dq[SH:])
+    hand_on(pl.ds(0, 1), 0, every)
 
     for pos, e in enumerate(ORDER):
         rows, keys = slice(pos * BLK, (pos + 1) * BLK), slice((6 + e) * BLK, (7 + e) * BLK)
@@ -428,12 +447,19 @@
     def spans(s):
         return {0: (0,), 7: (1,)}.get(s, (0, 1))
 
-    win_arrived(Q, far_oth, far_there)
+    def wait_sent(copies):
+        for c, when in copies:
+            if when is None:
+                c.wait_send()
+            else:
+                pl.when(when)(c.wait_send)
+
+    wait_sent(started[:early])
     for s in (0, 7, 2, 5, 1, 6):
         if s in (1, 6, 0, 7):
-            win_arrived(DO, s)
+            do_arrived(s)
         if s in (1, 2, 5, 6):
-            win_arrived(Q, s)
+            kvq_arrived(QQ, s)
         for c in spans(s):
             rows = slice(c * SH, (c + 1) * SH)
             KS[s, rows] = dot_t(WIN[K, 3 + c], WIN[Q, s]) * C2
@@ -459,12 +485,14 @@
                     TK[dst, s * SH : (s + 1) * SH] = (p * (KDP[s, src] - srd)).astype(BF16)
                     return carry
 
-                lax.fori_loop(0, BLK // 64, piece, 0)
+                lax.fori_loop(0, BLK // 64, piece, 0, unroll=True)
         rows = slice(part * SH, (part + 1) * SH)
         dk = (dot(TK[rows, :], WIN[Q].reshape(wide)) * SCALE).astype(BF16)
-        hand_over(1, part, dk[:BLK], dk[BLK:])
+        half = pl.ds(part * BLK, BLK)
+        hand_over(1, half, dk[:BLK], dk[BLK:])
         dv = dot(PK[rows, :], WIN[DO].reshape(wide)).astype(BF16)
-        hand_over(2, part, dv[:BLK], dv[BLK:])
+        hand_over(2, half, dv[:BLK], dv[BLK:])
+        hand_on(pl.ds(1, 2), 1 + part, half)
 
     def partial(part, step):
         rows = w_rows(step)
@@ -481,9 +509,10 @@
 
     kept = []
     for part in range(2):
-        for i in range(3):
-            rows = pl.ds(part * BLK, BLK)
-            arrived(GP.at[i, rows, oth_col], gs.at[i, part], gr.at[i, part])
+        if part == 0:
+            arrived(GP.at[pl.ds(0, 1), every, oth_col], gs.at[0], gr.at[0])
+        rows = pl.ds(part * BLK, BLK)
+        arrived(GP.at[pl.ds(1, 2), rows, oth_col], gs.at[1 + part], gr.at[1 + part])
         gx = partial(part, 2)
         pass_on(part, 0, gx[:HALF], right)
         pass_on(part, 1, gx[HALF:], left)
@@ -507,11 +536,7 @@
     store.start()
     att_own.wait()
     arrived(att.at[:, oth_col], as_.at[0], ar.at[0])
-    for c, when in started:
-        if when is None:
-            c.wait_send()
-        else:
-            pl.when(when)(c.wait_send)
+    wait_sent(started[early:])
     store.wait()
 
 
@@ -524,15 +549,12 @@
         hbm_spec = pl.BlockSpec(memory_space=pltpu.HBM)
         dma = pltpu.SemaphoreType.DMA
         vmem = pltpu.VMEM
-        return tuple(
+        out = (
             pl.pallas_call(
                 functools.partial(kernel, nctx, nhead),
-                out_shape=[
-                    jax.ShapeDtypeStruct((SH, SH), BF16),
-                    jax.ShapeDtypeStruct((SH, SH), BF16),
-                ],
+                out_shape=jax.ShapeDtypeStruct((2, SH, SH), BF16),
                 in_specs=[hbm_spec] * 4,
-                out_specs=[any_spec, any_spec],
+                out_specs=any_spec,
                 scratch_shapes=[
                     vmem((4, SH, SH), BF16),
                     vmem((3, 1024, SH), BF16),
@@ -560,13 +582,13 @@
                     vmem((2, 6, HALF, SH), BF16),
                     vmem((SH, SH), BF16),
                     vmem((4, SH, SH), BF16),
-                    vmem((4, SH, HD), BF16),
+                    vmem((3, SH, HD), BF16),
                     pltpu.SMEM((2, 9), jnp.int32),
                     dma((6,)),
                     dma((6,)),
                     dma((6,)),
-                    dma((7,)),
-                    dma((7,)),
+                    dma((8,)),
+                    dma((8,)),
                     dma((4, 7)),
                     dma((4, 8)),
                     dma((1,)),
@@ -575,8 +597,8 @@
                     dma((4,)),
                     dma((1,)),
                     dma((1,)),
-                    dma((3, 2)),
-                    dma((3, 2)),
+                    dma((3,)),
+                    dma((3,)),
                     dma((2, 6)),
                     dma((2, 6)),
                 ],
@@ -587,6 +609,7 @@
                 ),
             )(features, w, block_links, d_out)
         )
+        return out[0], out[1]
 
     return jax.shard_map(
         body,

time: 46.1 us -> 43.3 us (0.939)
  the two profiles are of different devices: /device:TPU:1 before, /device:TPU:250 now
where the time goes in v4:
time: 43.3 us; the launch traced here: 43.1 us
  Pallas kernels  40.8 us (94%)
  local copies, waits for them, and re-layouts  1.68 us (4%)
  between operations  0.64 us (1%)
    pallas_call x1, Pallas kernels, body(): pl.pallas_call(functools.partial(kernel, nctx, nhead), out_shape=jax.Shap...  40.8 us
    squeeze x1, local copies, waits for them, and re-layouts, body(): return (out[0], out[1])  1.68 us

profile of v4, /device:TPU:250, one launch (start us, length us, event | category | flops | bytes accessed | tf_op | source)
XLA Modules:
  0.0 43.1 jit_solution(5176259822074204757)
XLA Ops:
  0.6 40.8 %shard_map.59 = bf16[2,256,256]{2,1,0:T(8,128)(2,1)} custom-call(bf16[256,256]{1,0:T(8,128)(2,1)} %feat.1, bf16[3,1024,256]{2,1,0:T(8,128)(2,1)} %bitcast.5, s32[2,9]{1,0:T(2,128)} %links.1, bf16[256,256]{1,0:T(8,128)(2,1)} %dout.1), custom_call_target="tpu_custom_call" | custom-call | tf_op jit(solution)/shard_map/pallas_call | solution.py:553
  41.4 1.7 %slice_bitcast_fusion = (bf16[256,256]{1,0:T(8,128)(2,1)}, bf16[256,256]{1,0:T(8,128)(2,1)}) fusion(bf16[2,256,256]{2,1,0:T(8,128)(2,1)} %shard_map.59), kind=kLoop, calls=%fused_computation | loop fusion | bytes 524288 | tf_op jit(solution)/shard_map/squeeze | solution.py:612

commit v5 on v4

--- a/solution.py
+++ b/solution.py
@@ -66,6 +66,7 @@
     VT,
     STO,
     STI,
+    DKV,
     AST,
     GP,
     GST,
@@ -115,8 +116,6 @@
     A, B = pl.ds(0, BLK), pl.ds(BLK, BLK)
 
     att, gout = both.at[0], both.at[1]
-    load_l = pltpu.make_async_copy(links, LK, loc.at[5])
-    load_l.start()
     barrier = pltpu.get_barrier_semaphore()
     for peer in (right, left, partner):
         pl.semaphore_signal(barrier, inc=1, device_id=peer, device_id_type=MESH)
@@ -129,33 +128,14 @@
             for which in (0, 1):
                 pl.semaphore_signal(barrier, inc=1, device_id=at(d, which), device_id_type=MESH)
 
+    load_l = pltpu.make_async_copy(links, LK, loc.at[5])
+    load_l.start()
     load_f = pltpu.make_async_copy(feat, F.at[0], loc.at[0])
     load_f.start()
     load_w = pltpu.make_async_copy(w, W, loc.at[1])
     load_w.start()
     load_d = pltpu.make_async_copy(dout.at[:, own_col], WIN.at[DO, 3 + core], loc.at[2])
     load_d.start()
-
-    for d, n, slots in ((-2, 0, (0,)), (-1, 1, (1, 2)), (1, 2, (5, 6)), (2, 3, (7,))):
-
-        @pl.when(jnp.logical_not(has[d]))
-        def _():
-            for slot in slots:
-                for kind in range(4):
-                    WIN[kind, slot] = jnp.zeros((SH, HD), BF16)
-            STI[n, 0:4] = jnp.zeros((4, 2 * SH), F32)
-            STI[n, 4:8] = jnp.full((4, 2 * SH), DEAD, F32)
-
-    base = chip * 4 - 6 - PAD
-    row = lax.broadcasted_iota(jnp.int32, (ROWS, BLK), 0)
-    load_l.wait()
-    for r in range(2):
-        live = None
-        for j in range(9):
-            entry = LK[r, j]
-            hit = row == jnp.where(entry >= 0, entry - base, -1)
-            live = hit if live is None else live | hit
-        BQ[core, :, r * BLK : (r + 1) * BLK] = jnp.where(live, 0.0, DEAD).astype(F32)
 
     started = []
 
@@ -279,8 +259,29 @@
     mine.begin()
     out_two = ((core == 1) & has[2]) | ((core == 0) & has[-2])
     send(feat, FF.at[0], fs.at[6], fr.at[6], at(jnp.where(core == 1, 2, -2), oth), out_two)
+    send(dout.at[:, oth_col], WIN.at[DO, 3 + core], ws.at[DO, 0], wr.at[DO, 3 + core], partner)
+    for d, n, slots in ((-2, 0, (0,)), (-1, 1, (1, 2)), (1, 2, (5, 6)), (2, 3, (7,))):
+
+        @pl.when(jnp.logical_not(has[d]))
+        def _():
+            for slot in slots:
+                for kind in range(4):
+                    WIN[kind, slot] = jnp.zeros((SH, HD), BF16)
+            STI[n, 0:4] = jnp.zeros((4, 2 * SH), F32)
+            STI[n, 4:8] = jnp.full((4, 2 * SH), DEAD, F32)
+
+    base = chip * 4 - 6 - PAD
+    row = lax.broadcasted_iota(jnp.int32, (ROWS, BLK), 0)
+    load_l.wait()
+    for r in range(2):
+        live = None
+        for j in range(9):
+            entry = LK[r, j]
+            hit = row == jnp.where(entry >= 0, entry - base, -1)
+            live = hit if live is None else live | hit
+        BQ[core, :, r * BLK : (r + 1) * BLK] = jnp.where(live, 0.0, DEAD).astype(F32)
+
     send(BQ.at[core], BQ.at[core], bs.at[0], br.at[0], partner)
-    send(dout.at[:, oth_col], WIN.at[DO, 3 + core], ws.at[DO, 0], wr.at[DO, 3 + core], partner)
     for tab in (PB, DSB):
         tab[:SH, SH:] = jnp.zeros((SH, SH), BF16)
         tab[7 * SH :, :SH] = jnp.zeros((SH, SH), BF16)
@@ -307,7 +308,6 @@
     spread(QQ)
     far.pass_right()
     far.pass_left()
-    relay_do()
 
     partner_arrived(QQ)
     load_d.wait()
@@ -367,6 +367,7 @@
     r8 = l8
     m, l8, r8 = query_side(0, PAIRS[0], m, l8, r8)
 
+    relay_do()
     far.rest()
 
     @pl.when(far_here)
@@ -439,10 +440,11 @@
     hand_over(0, every, dq[:SH], dq[SH:])
     hand_on(pl.ds(0, 1), 0, every)
 
+    own_q, own_d = WIN[Q, 3:5].reshape(2 * SH, HD), WIN[DO, 3:5].reshape(2 * SH, HD)
     for pos, e in enumerate(ORDER):
         rows, keys = slice(pos * BLK, (pos + 1) * BLK), slice((6 + e) * BLK, (7 + e) * BLK)
-        PK[rows, 3 * SH : 5 * SH] = PB[keys, :]
-        TK[rows, 3 * SH : 5 * SH] = DSB[keys, :]
+        DKV[0, rows] = dot(DSB[keys, :], own_q)
+        DKV[1, rows] = dot(PB[keys, :], own_d)
 
     def spans(s):
         return {0: (0,), 7: (1,)}.get(s, (0, 1))
@@ -466,7 +468,6 @@
             KDP[s, rows] = dot_t(WIN[V, 3 + c], WIN[DO, s])
     for n, d in enumerate(FAR):
         arrived(STI.at[n], ss.at[n], sr.at[n], has[d])
-    wide = (8 * SH, HD)
     for part in range(2):
         for s in (2, 5, 1, 6, 0, 7):
             n, half = SOURCE[s]
@@ -487,10 +488,13 @@
 
                 lax.fori_loop(0, BLK // 64, piece, 0, unroll=True)
         rows = slice(part * SH, (part + 1) * SH)
-        dk = (dot(TK[rows, :], WIN[Q].reshape(wide)) * SCALE).astype(BF16)
+        lo, hi, side = slice(0, 3 * SH), slice(5 * SH, 8 * SH), (3 * SH, HD)
+        dk = DKV[0, rows] + dot(TK[rows, lo], WIN[Q, :3].reshape(side)) + dot(TK[rows, hi], WIN[Q, 5:].reshape(side))
+        dk = (dk * SCALE).astype(BF16)
         half = pl.ds(part * BLK, BLK)
         hand_over(1, half, dk[:BLK], dk[BLK:])
-        dv = dot(PK[rows, :], WIN[DO].reshape(wide)).astype(BF16)
+        dv = DKV[1, rows] + dot(PK[rows, lo], WIN[DO, :3].reshape(side)) + dot(PK[rows, hi], WIN[DO, 5:].reshape(side))
+        dv = dv.astype(BF16)
         hand_over(2, half, dv[:BLK], dv[BLK:])
         hand_on(pl.ds(1, 2), 1 + part, half)
 
@@ -575,6 +579,7 @@
                     vmem((HD, 8 * SH), BF16),
                     vmem((4, 8, 2 * SH), F32),
                     vmem((4, 8, 2 * SH), F32),
+                    vmem((2, 2 * SH, HD), F32),
                     vmem((2, SH, HD), BF16),
                     vmem((3, SH, SH), BF16),
                     vmem((3, SH, HD), BF16),

time: 43.3 us -> 43.2 us (level)
  the two profiles are of different devices: /device:TPU:250 before, /device:TPU:1 now
where the time goes in v5:
time: 43.2 us; the launch traced here: 42.6 us
  Pallas kernels  40.3 us (93%)
  local copies, waits for them, and re-layouts  1.68 us (4%)
  between operations  0.64 us (1%)
    pallas_call x1, Pallas kernels, body(): pl.pallas_call(functools.partial(kernel, nctx, nhead), out_shape=jax.Shap...  40.3 us
    squeeze x1, local copies, waits for them, and re-layouts, body(): return (out[0], out[1])  1.68 us

profile of v5, /device:TPU:1, one launch (start us, length us, event | category | flops | bytes accessed | tf_op | source)
XLA Modules:
  0.0 42.6 jit_solution(15112996870953899898)
XLA Ops:
  0.6 40.3 %shard_map.59 = bf16[2,256,256]{2,1,0:T(8,128)(2,1)} custom-call(bf16[256,256]{1,0:T(8,128)(2,1)} %feat.1, bf16[3,1024,256]{2,1,0:T(8,128)(2,1)} %bitcast.5, s32[2,9]{1,0:T(2,128)} %links.1, bf16[256,256]{1,0:T(8,128)(2,1)} %dout.1), custom_call_target="tpu_custom_call" | custom-call | tf_op jit(solution)/shard_map/pallas_call | solution.py:557
  41.0 1.7 %slice_bitcast_fusion = (bf16[256,256]{1,0:T(8,128)(2,1)}, bf16[256,256]{1,0:T(8,128)(2,1)}) fusion(bf16[2,256,256]{2,1,0:T(8,128)(2,1)} %shard_map.59), kind=kLoop, calls=%fused_computation | loop fusion | bytes 524288 | tf_op jit(solution)/shard_map/squeeze | solution.py:617

commit v6 on v5

--- a/solution.py
+++ b/solution.py
@@ -512,6 +512,7 @@
         return RSI[part, n].astype(F32)
 
     kept = []
+    stores = []
     for part in range(2):
         if part == 0:
             arrived(GP.at[pl.ds(0, 1), every, oth_col], gs.at[0], gr.at[0])
@@ -536,12 +537,14 @@
         start = part * BLK
         OUT[start : start + HALF] = (g_a + rs_arrived(part, 4)).astype(BF16)
         OUT[start + HALF : start + BLK] = (g_b + rs_arrived(part, 5)).astype(BF16)
-    store = pltpu.make_async_copy(OUT, gout, loc.at[4])
-    store.start()
+        rows = pl.ds(start, BLK)
+        stores.append(pltpu.make_async_copy(OUT.at[rows], gout.at[rows], loc.at[6 + part]))
+        stores[-1].start()
     att_own.wait()
     arrived(att.at[:, oth_col], as_.at[0], ar.at[0])
     wait_sent(started[early:])
-    store.wait()
+    for store in stores:
+        store.wait()
 
 
 def solution(mesh):
@@ -589,7 +592,7 @@
                     vmem((4, SH, SH), BF16),
                     vmem((3, SH, HD), BF16),
                     pltpu.SMEM((2, 9), jnp.int32),
-                    dma((6,)),
+                    dma((8,)),
                     dma((6,)),
                     dma((6,)),
                     dma((8,)),

time: 43.2 us -> 43.2 us (level)
  no operation moved by 1% of the time
where the time goes in v6:
time: 43.2 us; the launch traced here: 42.6 us
  Pallas kernels  40.3 us (93%)
  local copies, waits for them, and re-layouts  1.68 us (4%)
  between operations  0.64 us (1%)
    pallas_call x1, Pallas kernels, body(): pl.pallas_call(functools.partial(kernel, nctx, nhead), out_shape=jax.Shap...  40.3 us
    squeeze x1, local copies, waits for them, and re-layouts, body(): return (out[0], out[1])  1.68 us

profile of v6, /device:TPU:1, one launch (start us, length us, event | category | flops | bytes accessed | tf_op | source)
XLA Modules:
  0.0 42.6 jit_solution(14248137250237127543)
XLA Ops:
  0.6 40.3 %shard_map.59 = bf16[2,256,256]{2,1,0:T(8,128)(2,1)} custom-call(bf16[256,256]{1,0:T(8,128)(2,1)} %feat.1, bf16[3,1024,256]{2,1,0:T(8,128)(2,1)} %bitcast.5, s32[2,9]{1,0:T(2,128)} %links.1, bf16[256,256]{1,0:T(8,128)(2,1)} %dout.1), custom_call_target="tpu_custom_call" | custom-call | tf_op jit(solution)/shard_map/pallas_call | solution.py:560
  41.0 1.7 %slice_bitcast_fusion = (bf16[256,256]{1,0:T(8,128)(2,1)}, bf16[256,256]{1,0:T(8,128)(2,1)}) fusion(bf16[2,256,256]{2,1,0:T(8,128)(2,1)} %shard_map.59), kind=kLoop, calls=%fused_computation | loop fusion | bytes 524288 | tf_op jit(solution)/shard_map/squeeze | solution.py:620
